TPU v7x, 32 devices: a whole 2x2x4 slice. The times are simulated.
32 devices in a mesh: dp: 4 (over y, x), seq: 8 (over z, core).
Axes of the slice: x: 2, y: 2, z: 4, core: 2. Of those that a mesh axis runs over, the one named last changes fastest.
Arguments:
- tokens: bfloat16 [4, 1024, 512], P('dp', 'seq'), may hold values from -6 to 6
- doc_start: int32 [4, 1024], P('dp', 'seq'), may hold values from 0 to 1, as said below
- norm1_gain: float32 [512], replicated, may hold values from 0.1 to 1.9
- qkv_weight: bfloat16 [512, 1536], replicated, may hold values from -0.25 to 0.25
- out_weight: bfloat16 [512, 512], replicated, may hold values from -1 to 1
- norm2_gain: float32 [512], replicated, may hold values from 0.1 to 1.9
- up_weight: bfloat16 [512, 2048], replicated, may hold values from -0.25 to 0.25
- down_weight: bfloat16 [2048, 512], replicated, may hold values from -0.125 to 0.125
- omega: float32 [8, 64, 256], replicated, may hold values from -6 to 6
- cotangent: bfloat16 [4, 1024, 512], P('dp', 'seq'), may hold values from -6 to 6
Outputs:
- output: bfloat16 [4, 1024, 512], P('dp', 'seq')
- tokens_grad: float32 [4, 1024, 512], P('dp', 'seq')
- norm1_grad: float32 [512], replicated
- qkv_grad: float32 [512, 1536], replicated
- out_grad: float32 [512, 512], replicated
- norm2_grad: float32 [512], replicated
- up_grad: float32 [512, 2048], replicated
- down_grad: float32 [2048, 512], replicated
Inputs may be any that keep to these rules, and one draw needn't show every extreme that they name: `doc_start`: every row begins with 1. One row of all 4, drawn from the seed, holds a single document of the whole row; the other rows hold documents of mean length about 1024.
All inputs are finite; a program needn't handle non-finite values.
Results may differ from a plain program's by a relative error of at most 0.012.
The roundings to bfloat16 on the way count: a program that leaves them out, or rounds other values in their place, can miss the bound.
Values sent between devices are 32-bit elements; how exact they have to be, the bound alone decides.
No kernel may reach another device: no remote copies, remote signals or barrier semaphores. Data moves between devices by JAX's collectives and lax.ppermute only.
A program may use at most 192 MiB of HBM per device.

v0:
```python
import jax
import jax.numpy as jnp
from jax import lax
from jax.sharding import PartitionSpec as P

norm_eps = 1e-05
highest_precision = lax.Precision.HIGHEST


def entering(value, axis, join, neutral, backward):
    count, mine = (lax.axis_size(axis), lax.axis_index(axis))
    pieces = jax.tree.map(lambda part: lax.all_gather(part, axis), value)
    if backward:
        pieces = jax.tree.map(lambda part: part[::-1], pieces)
        mine = count - 1 - mine
    running = jax.tree.map(
        lambda part, zero: jnp.full_like(part, 0) + jnp.asarray(zero, part.dtype), value, neutral
    )

    def hop(position, running):
        longer = join(running, jax.tree.map(lambda part: part[position], pieces))
        return jax.tree.map(lambda new, old: jnp.where(position < mine, new, old), longer, running)

    return lax.fori_loop(0, count - 1, hop, running)


def layer_norm(values, gain):
    average = jnp.mean(values, axis=-1, keepdims=True)
    centred = values - average
    spread_sq = jnp.mean(centred * centred, axis=-1, keepdims=True)
    return centred * lax.rsqrt(spread_sq + norm_eps) * gain


def features(head_values, omega):
    width_dim = head_values.shape[-1]
    scaled = head_values * width_dim ** (-0.25)
    projection = jnp.einsum("...hd,hdm->...hm", scaled, omega, precision=highest_precision)
    half_square = 0.5 * jnp.sum(scaled * scaled, axis=-1, keepdims=True)
    return jnp.exp(projection - half_square)


def exact_gelu(values):
    return jax.nn.gelu(values, approximate=False)


def row_masks(doc_start):
    stretch_len = doc_start.shape[1]
    doc_index = jnp.cumsum(doc_start, axis=1)
    position = jnp.arange(stretch_len, dtype=jnp.int32)
    same_doc = (doc_index[:, :, None] == doc_index[:, None, :]) & (
        position[None, :, None] >= position[None, None, :]
    )
    leading_document = (doc_index == 0).astype(jnp.float32)
    last_doc = (doc_index == doc_index[:, -1:]).astype(jnp.float32)
    document_marker = (doc_index[:, -1] > 0).astype(jnp.float32)
    return (same_doc.astype(jnp.float32), leading_document, last_doc, document_marker)


def mix_rows(
    query_features, key_feat, value_heads, running_state, carry_norm, same_doc, leading_document
):
    scores = (
        jnp.einsum("rihm,rjhm->rhij", query_features, key_feat, precision=highest_precision)
        * same_doc[:, None]
    )
    attention_numerator = jnp.einsum(
        "rhij,rjhd->rihd", scores, value_heads, precision=highest_precision
    )
    attention_numerator = attention_numerator + leading_document[:, :, None, None] * jnp.einsum(
        "rihm,rhmd->rihd", query_features, running_state, precision=highest_precision
    )
    denominator = jnp.transpose(jnp.sum(scores, axis=-1), (0, 2, 1))
    denominator = denominator + leading_document[:, :, None] * jnp.einsum(
        "rihm,rhm->rih", query_features, carry_norm, precision=highest_precision
    )
    return attention_numerator / denominator[..., None]


def stretch_totals(key_feat, value_heads, last_doc):
    key_masked_rows = key_feat * last_doc[:, :, None, None]
    state_sum = jnp.einsum(
        "rchm,rchd->rhmd", key_masked_rows, value_heads, precision=highest_precision
    )
    return (state_sum, jnp.sum(key_masked_rows, axis=1))


def carry_on(earlier, later):
    state_sum, norm_sum, document_marker = later
    pass_on = 1.0 - document_marker
    return (
        state_sum + pass_on[:, None, None, None] * earlier[0],
        norm_sum + pass_on[:, None, None] * earlier[1],
        jnp.maximum(earlier[2], document_marker),
    )


def local(
    tokens,
    doc_start,
    norm1_gain,
    qkv_weight,
    out_weight,
    norm2_gain,
    up_weight,
    down_weight,
    omega,
    cotangent,
):
    row_count, stretch_len, model_width = tokens.shape
    head_count = omega.shape[0]
    head_dim = omega.shape[1]
    token_count = row_count * stretch_len
    stream = tokens.astype(jnp.float32).reshape(token_count, model_width)
    same_doc, leading_document, last_doc, document_marker = row_masks(doc_start)
    normed_one, norm1_back = jax.vjp(layer_norm, stream, norm1_gain)
    normed_one_low = normed_one.astype(jnp.bfloat16)
    projected = jnp.dot(normed_one_low, qkv_weight, preferred_element_type=jnp.float32)
    head_split = projected.reshape(row_count, stretch_len, 3, head_count, head_dim)
    query_heads = head_split[:, :, 0]
    key_heads = head_split[:, :, 1]
    value_heads = head_split[:, :, 2]

    def both_features(query_part, key_part):
        return (features(query_part, omega), features(key_part, omega))

    (query_features, key_feat), feature_back = jax.vjp(both_features, query_heads, key_heads)

    def local_totals(key_part, value_part):
        return stretch_totals(key_part, value_part, last_doc)

    (state_sum, norm_sum), totals_back = jax.vjp(local_totals, key_feat, value_heads)
    empty_state = jnp.zeros_like(state_sum)
    empty_norm = jnp.zeros_like(norm_sum)
    empty_flag = jnp.zeros_like(document_marker)
    running_state, carry_norm, unused_flag = entering(
        (state_sum, norm_sum, document_marker),
        "seq",
        carry_on,
        (empty_state, empty_norm, empty_flag),
        False,
    )

    def local_mix(query_part, key_part, value_part, state_part, norm_part):
        return mix_rows(
            query_part, key_part, value_part, state_part, norm_part, same_doc, leading_document
        )

    mixed, mix_back = jax.vjp(
        local_mix, query_features, key_feat, value_heads, running_state, carry_norm
    )
    mixed_low = mixed.reshape(token_count, model_width).astype(jnp.bfloat16)
    branch = jnp.dot(mixed_low, out_weight, preferred_element_type=jnp.float32)
    middle = stream + branch
    normed_two, norm2_back = jax.vjp(layer_norm, middle, norm2_gain)
    normed_two_low = normed_two.astype(jnp.bfloat16)
    up_values = jnp.dot(normed_two_low, up_weight, preferred_element_type=jnp.float32)
    gelu_out, gelu_back = jax.vjp(exact_gelu, up_values)
    hidden = gelu_out.astype(jnp.bfloat16)
    ffn_out = jnp.dot(hidden, down_weight, preferred_element_type=jnp.float32)
    output = (middle + ffn_out).astype(jnp.bfloat16).reshape(row_count, stretch_len, model_width)
    incoming = cotangent.reshape(token_count, model_width)
    down_grad = jnp.einsum("tf,td->fd", hidden, incoming, preferred_element_type=jnp.float32)
    hidden_grad = jnp.einsum("td,fd->tf", incoming, down_weight, preferred_element_type=jnp.float32)
    (up_full,) = gelu_back(hidden_grad)
    up_grad_low = up_full.astype(jnp.bfloat16)
    up_grad = jnp.einsum(
        "td,tf->df", normed_two_low, up_grad_low, preferred_element_type=jnp.float32
    )
    normed_two_grad = jnp.einsum(
        "tf,df->td", up_grad_low, up_weight, preferred_element_type=jnp.float32
    )
    middle_part, norm2_grad = norm2_back(normed_two_grad)
    middle_grad = incoming.astype(jnp.float32) + middle_part
    middle_low = middle_grad.astype(jnp.bfloat16)
    out_grad = jnp.einsum("td,te->de", mixed_low, middle_low, preferred_element_type=jnp.float32)
    mixed_grad = jnp.einsum("te,de->td", middle_low, out_weight, preferred_element_type=jnp.float32)
    mixed_grad = mixed_grad.reshape(row_count, stretch_len, head_count, head_dim)
    query_feat_grad, key_feat_mix, value_mix, carry_state_grad, carry_norm_grad = mix_back(
        mixed_grad
    )
    later_state, later_norm, unused_later = entering(
        (carry_state_grad, carry_norm_grad, document_marker),
        "seq",
        carry_on,
        (empty_state, empty_norm, empty_flag),
        True,
    )
    key_feat_tot, value_tot = totals_back((later_state, later_norm))
    query_grad, key_grad = feature_back((query_feat_grad, key_feat_mix + key_feat_tot))
    value_grad = value_mix + value_tot
    projected_grad = jnp.stack((query_grad, key_grad, value_grad), axis=2)
    projected_grad = projected_grad.reshape(token_count, 3 * model_width).astype(jnp.bfloat16)
    qkv_grad = jnp.einsum(
        "td,te->de", normed_one_low, projected_grad, preferred_element_type=jnp.float32
    )
    normed_one_grad = jnp.einsum(
        "te,de->td", projected_grad, qkv_weight, preferred_element_type=jnp.float32
    )
    stream_part, norm1_grad = norm1_back(normed_one_grad)
    tokens_grad = (middle_grad + stream_part).reshape(row_count, stretch_len, model_width)
    device_count = lax.axis_size("dp") * lax.axis_size("seq")
    qkv_sum, out_sum, up_sum, down_sum, norm1_sum, norm2_sum = lax.psum(
        (qkv_grad, out_grad, up_grad, down_grad, norm1_grad, norm2_grad), ("dp", "seq")
    )
    return (
        output,
        tokens_grad,
        norm1_sum / device_count,
        qkv_sum / device_count,
        out_sum / device_count,
        norm2_sum / device_count,
        up_sum / device_count,
        down_sum / device_count,
    )


def solution(mesh):
    placed = (
        P("dp", "seq", None),
        P("dp", "seq"),
        P(),
        P(),
        P(),
        P(),
        P(),
        P(),
        P(),
        P("dp", "seq", None),
    )
    return jax.shard_map(
        local,
        mesh=mesh,
        in_specs=placed,
        out_specs=(P("dp", "seq", None), P("dp", "seq", None), P(), P(), P(), P(), P(), P()),
        check_vma=False,
    )
```

profile of v0, /device:TPU:0, one launch (start us, length us, event | category | flops | bytes accessed | tf_op | source)
XLA Modules:
  0.0 501.8 jit_solution(18344170026993566355)
XLA Ops:
  11.8 2.6 copy.50
  14.4 2.1 convolution_bitcast_fusion
  17.3 2.2 multiply_reduce_fusion
  19.5 1.7 fusion.39
  23.3 18.5 %all-reduce = f32[8]{0:T(128)S(1)} all-reduce(f32[8]{0:T(128)S(1)} %bitcast_dynamic-update-slice_fusion), channel_id=1, replica_groups=mesh['dp'=4,'seq'=8] {'seq'}, use_global_device_ids=true, to_apply=%add | all-reduce | flops 8 | bytes 64
  41.8 14.4 %all-gather.1 = f32[64,256]{1,0:T(8,128)S(1)} all-gather(f32[8,256]{1,0:T(8,128)S(1)} %get-tuple-element.404), channel_id=3, replica_groups=mesh['dp'=4,'seq'=8] {'seq'}, dimensions={0}, use_global_device_ids=true | all-gather | bytes 73728 | tf_op jit(solution)/shard_map/all_gather | solution.py:12
  56.3 2.2 fusion.89
  59.5 2.2 fusion.138
  61.7 10.3 %all-gather.7.cloned.1.call-done = f32[64,256,64]{1,2,0:T(8,128)} async-done(((f32[8,256,64]{1,2,0:T(8,128)}), f32[64,256,64]{1,2,0:T(8,128)}) %all-gather.7.cloned.1.call-update) | async-done | bytes 4194320 | tf_op jit(solution)/shard_map/all_gather | solution.py:12
  72.0 51.2 %while.35 = (s32[]{:T(128)}, f32[1,8,256,64]{3,2,1,0:T(8,128)}, f32[1,8,256]{2,1,0:T(8,128)S(1)}, s32[]{:T(128)}, f32[8,1,8,256,64]{3,4,2,0,1:T(8,128)}, /*index...) while((s32[]{:T(128)}, f32[1,8,256,64]{3,2,1,0:T(8,128)}, ...), condition=%wide.region_7.8_spmd.clone, body=%wide.region_6.7_spmd.clone.sunk | while | flops 532485 | bytes 3694743 | solution.py:24
  73.3 1.9 constant_dynamic-slice_fusion.6
  75.1 1.4 copy.91
  76.5 1.8 fusion.177
  79.5 1.9 constant_dynamic-slice_fusion.6
  81.4 1.4 copy.91
  82.8 3.0 fusion.177
  87.0 1.9 constant_dynamic-slice_fusion.6
  88.9 1.4 copy.91
  90.3 3.0 fusion.177
  94.5 1.9 constant_dynamic-slice_fusion.6
  97.7 3.0 fusion.177
  102.0 1.9 constant_dynamic-slice_fusion.6
  105.2 3.0 fusion.177
  109.5 1.9 constant_dynamic-slice_fusion.6
  111.3 1.4 copy.91
  112.7 3.0 fusion.177
  116.9 1.9 constant_dynamic-slice_fusion.6
  120.2 3.0 fusion.177
  123.2 2.4 fusion.50
  125.6 3.6 fusion.8
  129.8 2.2 divide_convert_fusion
  132.7 3.7 multiply_convert_fusion
  137.4 1.4 multiply_reduce_fusion.3
  141.3 1.7 convolution_bitcast_fusion.1
  146.6 1.4 fusion.45
  148.1 15.4 %all-gather.3 = f32[64,256]{1,0:T(8,128)} all-gather(f32[8,256]{1,0:T(8,128)S(1)} %bitcast.453), channel_id=5, replica_groups=mesh['dp'=4,'seq'=8] {'seq'}, dimensions={0}, use_global_device_ids=true | all-gather | bytes 73728 | tf_op jit(solution)/shard_map/all_gather | solution.py:12
  163.5 1.5 rev.11
  166.3 2.0 fusion.4
  168.4 2.3 convolution_add_fusion.1
  170.8 1.6 fusion.25
  172.5 3.2 fusion.11
  176.9 2.7 fusion.95
  179.6 2.8 fusion.131
  182.5 7.2 %all-gather.9.cloned.1.call-done = f32[8,8,256,64]{2,3,1,0:T(8,128)} async-done(((f32[1,8,256,64]{2,3,1,0:T(8,128)}), f32[8,8,256,64]{2,3,1,0:T(8,128)}) %all-gather.9.cloned.1.call-update) | async-done | bytes 4194320 | tf_op jit(solution)/shard_map/all_gather | solution.py:12
  189.7 4.7 reverse_bitcast_fusion
  194.4 43.2 %while.36 = (s32[]{:T(128)}, f32[1,8,256,64]{3,2,1,0:T(8,128)}, f32[1,8,256]{2,1,0:T(8,128)S(1)}, s32[]{:T(128)}, f32[8,1,8,256,64]{3,4,2,0,1:T(8,128)}, /*index...) while((s32[]{:T(128)}, f32[1,8,256,64]{3,2,1,0:T(8,128)}, ...), condition=%wide.region_16.17_spmd.clone, body=%wide.region_15.16_spmd.clone.sunk | while | flops 532485 | bytes 3694743 | solution.py:24
  197.8 1.7 fusion.180
  202.9 3.0 fusion.180
  209.2 3.0 fusion.180
  215.6 3.0 fusion.180
  221.9 3.0 fusion.180
  228.3 3.0 fusion.180
  234.6 3.0 fusion.180
  237.6 3.8 fusion.31
  241.4 2.4 fusion.33
  245.0 1.5 fusion.22
  246.6 2.6 fusion.14
  249.2 2.3 fusion.101
  252.6 2.8 fusion.16
  256.5 40.8 %all-reduce.1 = (f32[512]{0:T(512)S(1)}, f32[512]{0:T(512)S(1)}) all-reduce(f32[512]{0:T(512)S(1)} %get-tuple-element.356, f32[512]{0:T(512)S(1)} %copy-done.62), channel_id=1, replica_groups=mesh['dp'=4,'seq'=8] {'dp','seq'}, use_global_device_ids=true, to_apply=%region_21.22 | all-reduce | flops 1024 | bytes 8192 | tf_op jit(solution)/shard_map/psum | solution.py:202
  299.3 184.7 %all-reduce.5.cloned.1.call-done = (f32[512,1536]{1,0:T(8,128)}, f32[512,512]{1,0:T(8,128)}, f32[512,2048]{1,0:T(8,128)}, f32[2048,512]{1,0:T(8,128)}) async-done(((f32[512,1536]{1,0:T(8,128)}, f32[512,512]{1,0:T(8,128)}, f32[512,2048]{1,0:T(8,128)}, f32[2048,512]{1,0:T(8,128)}), (f32[512,1536]{1,0:T(8,128)}, f32[512,512]{1,0:T(8,128)}, f32[512,2048]{1,0:T(8,128)}, ...) | async-done | bytes 12582928 | tf_op jit(solution)/shard_map/psum | solution.py:202
  484.0 4.0 broadcast_multiply_fusion.2
  489.1 2.5 broadcast_multiply_fusion.1
  492.8 2.5 broadcast_multiply_fusion
  (246 shorter events, 62.5 us)
Async XLA Ops:
  7.2 125.5 %copy-start = (bf16[512,2048]{1,0:T(8,128)(2,1)S(1)}, bf16[512,2048]{1,0:T(8,128)(2,1)}, u32[]{:S(2)}) copy-start(bf16[512,2048]{1,0:T(8,128)(2,1)} %param.20) | copy-start | bytes 6291460
  7.2 7.2 %copy-start.11 = (bf16[1,128,512]{2,1,0:T(8,128)(2,1)S(1)}, bf16[1,128,512]{2,1,0:T(8,128)(2,1)}, u32[]{:S(2)}) copy-start(bf16[1,128,512]{2,1,0:T(8,128)(2,1)} %param.14) | copy-start | bytes 393220
  7.2 7.2 %copy-start.48 = (f32[512]{0:T(512)S(1)}, f32[512]{0:T(512)}, u32[]{:S(2)}) copy-start(f32[512]{0:T(512)} %param.16) | copy-start | bytes 6148
  7.2 64.8 %all-gather.7.cloned.1.call-start = ((), (), s32[]{:S(2)}) async-start(), calls=%async_computation | async-start | bytes 4718592 | tf_op jit(solution)/shard_map/all_gather | solution.py:12
  10.0 6.6 %copy-start.54 = (f32[128]{0:T(128)}, f32[128]{0:T(128)S(1)}, u32[]{:S(2)}) copy-start(f32[128]{0:T(128)S(1)} %broadcast_multiply_fusion.9) | copy-start | bytes 1540
  11.1 3.3 copy-start.69
  11.1 3.3 copy-start.63
  11.7 7.8 %copy-start.56 = (f32[128]{0:T(128)}, f32[128]{0:T(128)S(1)}, u32[]{:S(2)}) copy-start(f32[128]{0:T(128)S(1)} %get-tuple-element.403) | copy-start | bytes 1540
  11.8 117.4 %copy-start.50 = (f32[128]{0:T(128)}, f32[128]{0:T(128)S(1)}, u32[]{:S(2)}) copy-start(f32[128]{0:T(128)S(1)} %get-tuple-element.402) | copy-start | bytes 1540
  14.4 7.6 %copy-start.73 = (u32[32]{0:T(128)S(1)}, u32[32]{0:T(128)}, u32[]{:S(2)}) copy-start(u32[32]{0:T(128)} %constant.176) | copy-start | bytes 388
  16.5 3.1 copy-start.8
  17.3 44.4 %copy-start.42 = (f32[128,8]{0,1:T(8,128)}, f32[128,8]{0,1:T(8,128)S(1)}, u32[]{:S(2)}) copy-start(f32[128,8]{0,1:T(8,128)S(1)} %get-tuple-element.420) | copy-start | bytes 12292
  17.3 122.9 %copy-start.39 = (f32[128,8]{0,1:T(8,128)}, f32[128,8]{0,1:T(8,128)S(1)}, u32[]{:S(2)}) copy-start(f32[128,8]{0,1:T(8,128)S(1)} %get-tuple-element.399) | copy-start | bytes 12292
  19.5 42.2 %copy-start.5 = (f32[8,128,256]{2,1,0:T(8,128)}, f32[8,128,256]{2,1,0:T(8,128)S(1)}, u32[]{:S(2)}) copy-start(f32[8,128,256]{2,1,0:T(8,128)S(1)} %get-tuple-element.405) | copy-start | bytes 3145732
  21.3 168.4 %all-gather.9.cloned.1.call-start = ((), (), s32[]{:S(2)}) async-start(), calls=%async_computation.1 | async-start | bytes 4718592 | tf_op jit(solution)/shard_map/all_gather | solution.py:12
  56.3 15.7 %copy-start.38 = (f32[128,128]{0,1:T(8,128)}, f32[128,128]{0,1:T(8,128)S(1)}, u32[]{:S(2)}) copy-start(f32[128,128]{0,1:T(8,128)S(1)} %fusion.112) | copy-start | bytes 196612
  123.2 8.8 %copy-start.71 = (f32[8,1]{0,1:T(1,128)}, f32[8,1]{0,1:T(1,128)S(1)}, u32[]{:S(2)}) copy-start(f32[8,1]{0,1:T(1,128)S(1)} %get-tuple-element.588) | copy-start | bytes 100
  123.2 6.6 %copy-start.15 = (f32[8,128,128]{1,2,0:T(8,128)S(1)}, f32[8,128,128]{1,2,0:T(8,128)}, u32[]{:S(2)}) copy-start(f32[8,128,128]{1,2,0:T(8,128)} %get-tuple-element.407) | copy-start | bytes 1572868
  123.2 8.8 %copy-start.24 = (bf16[512,512]{1,0:T(8,128)(2,1)S(1)}, bf16[512,512]{1,0:T(8,128)(2,1)}, u32[]{:S(2)}) copy-start(bf16[512,512]{1,0:T(8,128)(2,1)} %param.18) | copy-start | bytes 1572868
  123.2 9.5 %copy-start.52 = (f32[512]{0:T(512)S(1)}, f32[512]{0:T(512)}, u32[]{:S(2)}) copy-start(f32[512]{0:T(512)} %param.19) | copy-start | bytes 6148
  129.8 10.4 %copy-start.45 = (f32[128,8]{0,1:T(8,128)}, f32[128,8]{0,1:T(8,128)S(1)}, u32[]{:S(2)}) copy-start(f32[128,8]{0,1:T(8,128)S(1)} %get-tuple-element.393) | copy-start | bytes 12292
  132.4 6.5 %copy-start.60 = (f32[128]{0:T(128)}, f32[128]{0:T(128)S(1)}, u32[]{:S(2)}) copy-start(f32[128]{0:T(128)S(1)} %broadcast_multiply_fusion.8) | copy-start | bytes 1540
  132.7 6.2 %copy-start.65 = (f32[128]{0:T(128)}, f32[128]{0:T(128)S(1)}, u32[]{:S(2)}) copy-start(f32[128]{0:T(128)S(1)} %fusion.117) | copy-start | bytes 1540
  132.7 3.7 copy-start.23
  132.7 3.7 copy-start.31
  137.4 2.9 copy-start.21
  137.4 3.9 copy-start.3
  137.4 3.9 copy-start.51
  139.9 28.5 %copy-start.4 = (f32[1,8,256,64]{3,2,1,0:T(8,128)S(1)}, f32[1,8,256,64]{3,2,1,0:T(8,128)}, u32[]{:S(2)}) copy-start(f32[1,8,256,64]{3,2,1,0:T(8,128)} %get-tuple-element.258) | copy-start | bytes 1572868
  142.9 27.8 %copy-start.6 = (f32[8,128,256]{2,1,0:T(8,128)S(1)}, f32[8,128,256]{2,1,0:T(8,128)}, u32[]{:S(2)}) copy-start(f32[8,128,256]{2,1,0:T(8,128)} %copy-done.5) | copy-start | bytes 3145732
  143.0 341.1 %all-reduce.5.cloned.1.call-start = ((), (), s32[]{:S(2)}) async-start(), calls=%async_computation.2 | async-start | bytes 25165824 | tf_op jit(solution)/shard_map/psum | solution.py:202
  164.9 5.8 %copy-start.40 = (f32[128,8]{0,1:T(8,128)S(1)}, f32[128,8]{0,1:T(8,128)}, u32[]{:S(2)}) copy-start(f32[128,8]{0,1:T(8,128)} %copy-done.39) | copy-start | bytes 12292
  164.9 5.8 %copy-start.43 = (f32[128,8]{0,1:T(8,128)S(1)}, f32[128,8]{0,1:T(8,128)}, u32[]{:S(2)}) copy-start(f32[128,8]{0,1:T(8,128)} %copy-done.42) | copy-start | bytes 12292
  168.3 4.0 copy-start.27
  168.4 4.1 copy-start.9
  168.4 4.1 copy-start.58
  170.8 4.9 copy-start.30
  170.8 4.8 copy-start.35
  172.4 4.5 copy-start.25
  172.4 4.5 copy-start.32
  175.6 4.0 copy-start.22
  175.6 4.0 copy-start.53
  175.6 4.0 copy-start.61
  175.6 4.0 copy-start.66
  182.5 11.9 %copy-start.72 = (f32[8]{0:T(128)S(1)}, f32[8]{0:T(128)}, u32[]{:S(2)}) copy-start(f32[8]{0:T(128)} %reverse.1) | copy-start | bytes 100
  194.4 43.2 %copy-start.44 = (f32[128,8]{0,1:T(8,128)S(1)}, f32[128,8]{0,1:T(8,128)}, u32[]{:S(2)}) copy-start(f32[128,8]{0,1:T(8,128)} %copy-done.42) | copy-start | bytes 12292
  194.4 43.2 %copy-start.57 = (f32[128]{0:T(128)S(1)}, f32[128]{0:T(128)}, u32[]{:S(2)}) copy-start(f32[128]{0:T(128)} %copy-done.56) | copy-start | bytes 1540
  237.6 6.2 %copy-start.13 = (f32[128,512]{0,1:T(8,128)S(1)}, f32[128,512]{0,1:T(8,128)}, u32[]{:S(2)}) copy-start(f32[128,512]{0,1:T(8,128)} %copy-done.12) | copy-start | bytes 786436
  237.6 6.2 %copy-start.16 = (f32[8,128,128]{1,2,0:T(8,128)S(1)}, f32[8,128,128]{1,2,0:T(8,128)}, u32[]{:S(2)}) copy-start(f32[8,128,128]{1,2,0:T(8,128)} %get-tuple-element.407) | copy-start | bytes 1572868
  237.6 6.2 %copy-start.46 = (f32[128,8]{0,1:T(8,128)S(1)}, f32[128,8]{0,1:T(8,128)}, u32[]{:S(2)}) copy-start(f32[128,8]{0,1:T(8,128)} %copy-done.45) | copy-start | bytes 12292
  237.6 7.4 %copy-start.7 = (f32[8,128,256]{2,1,0:T(8,128)S(1)}, f32[8,128,256]{2,1,0:T(8,128)}, u32[]{:S(2)}) copy-start(f32[8,128,256]{2,1,0:T(8,128)} %copy-done.5) | copy-start | bytes 3145732
  237.6 7.4 %copy-start.28 = (f32[8,128,128]{1,2,0:T(8,128)S(1)}, f32[8,128,128]{1,2,0:T(8,128)}, u32[]{:S(2)}) copy-start(f32[8,128,128]{1,2,0:T(8,128)} %copy-done.27) | copy-start | bytes 1572868
  237.6 7.4 %copy-start.41 = (f32[128,8]{0,1:T(8,128)S(1)}, f32[128,8]{0,1:T(8,128)}, u32[]{:S(2)}) copy-start(f32[128,8]{0,1:T(8,128)} %copy-done.39) | copy-start | bytes 12292
  243.8 2.7 copy-start.10
  252.6 2.9 copy-start.14
  252.6 3.6 copy-start.70
  252.6 3.9 copy-start.62
  252.6 45.8 %copy-start.20 = (f32[128,512]{1,0:T(8,128)S(1)}, f32[128,512]{1,0:T(8,128)}, u32[]{:S(2)}) copy-start(f32[128,512]{1,0:T(8,128)} %copy-done.19) | copy-start | bytes 786436
  252.6 45.8 %copy-start.33 = (bf16[1,128,512]{2,1,0:T(8,128)(2,1)S(1)}, bf16[1,128,512]{2,1,0:T(8,128)(2,1)}, u32[]{:S(2)}) copy-start(bf16[1,128,512]{2,1,0:T(8,128)(2,1)} %param.23) | copy-start | bytes 393220
  252.6 45.8 %copy-start.68 = (f32[128]{0:T(128)S(1)}, f32[128]{0:T(128)}, u32[]{:S(2)}) copy-start(f32[128]{0:T(128)} %copy-done.67) | copy-start | bytes 1540
  484.0 4.0 copy-start.36
  484.0 5.0 %copy-start.18 = (f32[512,2048]{1,0:T(8,128)S(1)}, f32[512,2048]{1,0:T(8,128)}, u32[]{:S(2)}) copy-start(f32[512,2048]{1,0:T(8,128)} %get-tuple-element.390) | copy-start | bytes 12582916
  489.1 3.7 copy-start.17
  491.5 3.8 copy-start.1
  (13 other events, 19.9 us)
Sparse Core Ops, SparseCore 0:
  21.4 50.5 all-gather.6
  143.1 46.5 all-gather.8
  251.7 232.2 all-reduce.4
where the time goes:
time: 505 us; the launch traced here: 502 us
  waiting for transfers between devices  202 us (40%)
  blocking collectives  89.1 us (18%)
  other arithmetic  82.8 us (16%)
  matrix products  61.6 us (12%)
  local copies, waits for them, and re-layouts  50.4 us (10%)
  between operations  15.3 us (3%)
    psum x1, waiting for transfers between devices, local(): lax.psum((qkv_grad, out_grad, up_grad, down_grad, norm1_grad, norm2_grad)...  185 us
    select_n x28, other arithmetic, hop(): jnp.where(position < mine, new, old)  53.1 us
    psum x1, blocking collectives, local(): lax.psum((qkv_grad, out_grad, up_grad, down_grad, norm1_grad, norm2_grad)...  40.8 us
    dynamic_slice x28, local copies, waits for them, and re-layouts, hop(): longer = join(running, jax.tree.map(lambda part: part[position], pieces))  32.5 us
    all_gather x2, blocking collectives, entering(): pieces = jax.tree.map(lambda part: lax.all_gather(part, axis), value)  29.8 us
    unnamed x1, blocking collectives  18.5 us
    all_gather x2, waiting for transfers between devices, entering(): pieces = jax.tree.map(lambda part: lax.all_gather(part, axis), value)  17.5 us
    unnamed x153, local copies, waits for them, and re-layouts  11.1 us
  transfers between devices with their start and end apart: 3, of which 3 were waited for; matrix products, arithmetic and copies ran while one was open for 7% of the time, Pallas kernels for 0%

commit v1 on v0

--- a/solution.py
+++ b/solution.py
@@ -1,6 +1,10 @@
+import functools
+
 import jax
 import jax.numpy as jnp
 from jax import lax
+from jax.experimental import pallas as pl
+from jax.experimental.pallas import tpu as pltpu
 from jax.sharding import PartitionSpec as P
 
 norm_eps = 1e-05
@@ -214,6 +218,550 @@
     )
 
 
+eps = 1e-05
+f32 = jnp.float32
+bf16 = jnp.bfloat16
+AXES = ("dp", "seq")
+GRID_DP, GRID_SEQ = 4, 8
+ROOM = 56 * 2**20
+
+
+def place(y, x, z, c):
+    return (y * 2 + x) * GRID_SEQ + z * 2 + c
+
+
+def pairs(move):
+    return [
+        (place(y, x, z, c), place(*move(y, x, z, c)))
+        for y in range(2)
+        for x in range(2)
+        for z in range(4)
+        for c in range(2)
+    ]
+
+
+ALONG_Z = {k: pairs(lambda y, x, z, c, k=k: (y, x, z ^ k, c)) for k in (1, 2, 3)}
+CORES = pairs(lambda y, x, z, c: (y, x, z, 1 - c))
+FIRST = pairs(lambda y, x, z, c: (y, 1 - x, z, c) if c == 0 else (1 - y, x, z, c))
+SECOND = pairs(lambda y, x, z, c: (1 - y, x, z, c) if c == 0 else (y, 1 - x, z, c))
+
+
+def send(value, perm):
+    return lax.ppermute(value, AXES, perm)
+
+
+def nn(a, b, precision=None):
+    return lax.dot_general(
+        a, b, (((1,), (0,)), ((), ())), precision=precision, preferred_element_type=f32
+    )
+
+
+def nt(a, b, precision=None):
+    return lax.dot_general(
+        a, b, (((1,), (1,)), ((), ())), precision=precision, preferred_element_type=f32
+    )
+
+
+def work(micros):
+    return pl.CostEstimate(flops=int(micros * 1e9), bytes_accessed=0, transcendentals=0)
+
+
+def kernel_call(body, outs, ids, args, scratch=(), name=None, micros=2):
+    vmem = pl.BlockSpec(memory_space=pltpu.VMEM)
+    return pl.pallas_call(
+        body,
+        out_shape=[jax.ShapeDtypeStruct(s, d) for s, d in outs],
+        in_specs=[pl.BlockSpec(memory_space=pltpu.SMEM)] + [vmem] * len(args),
+        out_specs=[vmem] * len(outs),
+        scratch_shapes=list(scratch),
+        compiler_params=pltpu.CompilerParams(vmem_limit_bytes=ROOM),
+        name=name,
+        cost_estimate=work(micros),
+    )(ids, *args)
+
+
+def normalise(v):
+    mean = jnp.mean(v, axis=-1, keepdims=True)
+    centred = v - mean
+    inv = lax.rsqrt(jnp.mean(centred * centred, axis=-1, keepdims=True) + eps)
+    return centred * inv, inv
+
+
+def normalise_back(e, n, inv):
+    return (e - jnp.mean(e, axis=-1, keepdims=True) - n * jnp.mean(e * n, axis=-1, keepdims=True)) * inv
+
+
+def doc_numbers(doc):
+    at = lax.broadcasted_iota(jnp.int32, (128, 128), 0)
+    to = lax.broadcasted_iota(jnp.int32, (128, 128), 1)
+    upper = (at <= to).astype(f32)
+    a8 = lax.broadcasted_iota(jnp.int32, (8, 8), 0)
+    t8 = lax.broadcasted_iota(jnp.int32, (8, 8), 1)
+    before = (t8 < a8).astype(f32)
+    spread = jnp.broadcast_to(jnp.sum(doc, axis=1, keepdims=True), (8, 128))
+    high = lax.Precision.HIGHEST
+    rows = nn(doc, upper, high) + nn(before, spread, high)
+    eye = (at == to).astype(f32)
+    cols = nt(eye, rows, high)
+    return rows, cols
+
+
+def row_of(rows, lo, hi):
+    return jnp.concatenate([rows[j : j + 1, :] for j in range(lo, hi)], axis=1)
+
+
+def col_of(cols, lo, hi):
+    return jnp.concatenate([cols[:, j : j + 1] for j in range(lo, hi)], axis=0)
+
+
+def gelu_parts(u):
+    e = jnp.exp(-0.5 * u * u)
+    base = 1.0 + (0.3275911 * 0.7071067811865476) * jnp.abs(u)
+    t = pl.reciprocal(base, approx=True)
+    t = t * (2.0 - base * t)
+    tail = t * (
+        0.5 * 0.254829592
+        + t * (-0.5 * 0.284496736 + t * (0.5 * 1.421413741 + t * (-0.5 * 1.453152027 + t * (0.5 * 1.061405429))))
+    ) * e
+    return jnp.where(u < 0, tail, 1.0 - tail), e * 0.3989422804014327
+
+
+def head_forward(ids, t0, t1, t2, t3, p0, p1, p2, p3, gain, wh, omega,
+                 keep, give, phq_o, phk_o, qk_o, v_o, mxd_o, doc_o, nt_o, low):
+    z, c = ids[0], ids[1]
+    g = gain[...]
+    for k, (mine, theirs) in enumerate(((t0, p0), (t1, p1), (t2, p2), (t3, p3))):
+        for ref, core in ((mine, c), (theirs, 1 - c)):
+            chunk = 2 * jnp.bitwise_xor(z, k) + core
+            n, _ = normalise(ref[0:128, :])
+            low[pl.ds(pl.multiple_of(chunk * 128, 128), 128), :] = (n * g).astype(bf16)
+            doc_o[pl.ds(chunk, 1), :] = ref[128:129, 0:128]
+    rows, cols = doc_numbers(doc_o[...])
+    nt_o[...] = jnp.transpose(low[:, pl.ds(pl.multiple_of(c * 256, 256), 256)])
+    s = 64 ** -0.25
+    om = omega[...]
+    oh = om.astype(bf16)
+    ol = (om - oh.astype(f32)).astype(bf16)
+    stack = jnp.concatenate([oh, oh, ol], axis=0)
+
+    def feature(v):
+        v = v * s
+        hi = v.astype(bf16)
+        lo = (v - hi.astype(f32)).astype(bf16)
+        proj = nn(jnp.concatenate([hi, lo, hi], axis=1), stack)
+        return jnp.exp(proj - 0.5 * jnp.sum(v * v, axis=-1, keepdims=True))
+
+    for b in range(4):
+        at = pl.ds(256 * b, 256)
+        pr = nn(low[at, :], wh[...])
+        qk_o[at, :] = pr[:, 0:128]
+        v_o[at, :] = pr[:, 128:192].astype(bf16)
+        phq_o[at, :] = feature(pr[:, 0:64]).astype(bf16)
+        phk_o[at, :] = feature(pr[:, 64:128]).astype(bf16)
+    for b in range(4):
+        at = pl.ds(256 * b, 256)
+        n = 256 * (b + 1)
+        scores = nt(phq_o[at, :], phk_o[0:n, :])
+        i = lax.broadcasted_iota(jnp.int32, (256, n), 0) + 256 * b
+        j = lax.broadcasted_iota(jnp.int32, (256, n), 1)
+        same = (col_of(cols, 2 * b, 2 * b + 2) == row_of(rows, 0, 2 * b + 2)) & (i >= j)
+        scores = jnp.where(same, scores, 0.0)
+        inv = 1.0 / jnp.sum(scores, axis=-1, keepdims=True)
+        mixed = nn(scores.astype(bf16), v_o[0:n, :]) * inv
+        mxd_o[at, :] = jnp.concatenate([mixed, jnp.broadcast_to(inv, (256, 64))], axis=1)
+        top, bottom = mixed[0:128, :], mixed[128:256, :]
+        keep[b] = jnp.where(c == 0, top, bottom)
+        give[b] = jnp.where(c == 0, bottom, top)
+
+
+def pack_pairs(ids, keep, got, b0, b1, b2, b3):
+    z, c = ids[0], ids[1]
+    for k, out in enumerate((b0, b1, b2, b3)):
+        j = jnp.bitwise_xor(z, k)
+        a, b = keep[j], got[j]
+        out[...] = jnp.where(c == 0, jnp.concatenate([a, b], axis=1), jnp.concatenate([b, a], axis=1))
+
+
+def unpack_pairs(ids, b0, b1, b2, b3, keep, give):
+    z, c = ids[0], ids[1]
+    for k, ref in enumerate((b0, b1, b2, b3)):
+        j = jnp.bitwise_xor(z, k)
+        a, b = ref[:, 0:64], ref[:, 64:128]
+        keep[j] = jnp.where(c == 0, a, b)
+        give[j] = jnp.where(c == 0, b, a)
+
+
+def middle_part(ids, b0, b1, b2, b3, tokens, wo, gain, mixed_o, middle_o, normed_o):
+    z = ids[0]
+    for k, ref in enumerate((b0, b1, b2, b3)):
+        j = jnp.bitwise_xor(z, k)
+        mixed_o[:, pl.ds(pl.multiple_of(j * 128, 128), 128)] = ref[...].astype(bf16)
+    middle = tokens[...].astype(f32) + nn(mixed_o[...], wo[...])
+    middle_o[...] = middle
+    n, _ = normalise(middle)
+    normed_o[...] = (n * gain[...]).astype(bf16).astype(f32)
+
+
+def feed_forward(ids, mixed, middle, normed, cot, wu, wd, wo, gain,
+                 out_o, mg_o, ml_o, ex_o, b0, b1, b2, b3, scr):
+    z, c = ids[0], ids[1]
+    x = normed[...].astype(bf16)
+    inc = cot[...]
+    total = middle[...]
+    back = jnp.zeros((128, 512), f32)
+    for u in range(4):
+        at = pl.ds(512 * u, 512)
+        wub, wdb = wu[:, at], wd[at, :]
+        up = nn(x, wub)
+        cdf, pdf = gelu_parts(up)
+        total = total + nn((up * cdf).astype(bf16), wdb)
+        ug = ((cdf + up * pdf) * nt(inc, wdb)).astype(bf16)
+        back = back + nt(ug, wub)
+    out_o[...] = total.astype(bf16)
+    n, inv = normalise(middle[...])
+    mg = inc.astype(f32) + normalise_back(gain[...] * back, n, inv)
+    mg_o[...] = mg
+    low = mg.astype(bf16)
+    ml_o[...] = low
+    ex_o[:, 0:256] = mixed[:, pl.ds(pl.multiple_of((1 - c) * 256, 256), 256)].astype(f32)
+    ex_o[:, 256:768] = low.astype(f32)
+    scr[...] = nt(low, wo[...])
+    for k, ref in enumerate((b0, b1, b2, b3)):
+        j = jnp.bitwise_xor(z, k)
+        ref[...] = scr[:, pl.ds(pl.multiple_of(j * 128, 128), 128)]
+
+
+def out_part(ids, mixed, mlow, got, keep, give, scr):
+    c, first = ids[1], ids[2]
+    mine = mixed[:, pl.ds(pl.multiple_of(c * 256, 256), 256)].astype(f32)
+    left = jnp.transpose(jnp.concatenate([mine, got[:, 0:256]], axis=0)).astype(bf16)
+    right = jnp.concatenate([mlow[...], got[:, 256:768].astype(bf16)], axis=0)
+    scr[...] = nn(left, right)
+    keep[...] = scr[pl.ds(pl.multiple_of(first * 128, 128), 128), :]
+    give[...] = scr[pl.ds(pl.multiple_of((1 - first) * 128, 128), 128), :]
+
+
+def add_spread(ids, mine, got, o0, o1, o2, o3, scr):
+    scr[...] = mine[...] + got[...]
+    for k, ref in enumerate((o0, o1, o2, o3)):
+        j = jnp.bitwise_xor(ids[0], k)
+        ref[...] = scr[:, pl.ds(pl.multiple_of(j * 128, 128), 128)]
+
+
+def add_last(ids, mine, got, o0, o1, o2, o3, out):
+    out[:, 0:384] = (mine[...] + got[...]) * (1.0 / 32)
+    out[:, 384:512] = ((o0[...] + o1[...]) + (o2[...] + o3[...])) * (1.0 / 32)
+
+
+def head_backward(ids, keep, got, phq, phk, qk, v, mxd, doc, omega, pg_o, r_scr, m_scr):
+    c = ids[1]
+    for b in range(4):
+        a, g = keep[b], got[b]
+        at = pl.ds(256 * b, 256)
+        dm = jnp.concatenate([jnp.where(c == 0, a, g), jnp.where(c == 0, g, a)], axis=0)
+        r = dm * mxd[at, 64:128]
+        r_scr[at, :] = r.astype(bf16)
+        m_scr[at, :] = r * mxd[at, 0:64]
+    rows, cols = doc_numbers(doc[...])
+    ones = jnp.ones((8, 64), f32)
+    s = 64 ** -0.25
+    om = omega[...].astype(bf16)
+
+    def feature_back(ph, grad, base):
+        a = ph.astype(f32) * grad
+        return s * nt(a.astype(bf16), om) - (s * s) * base * jnp.sum(a, axis=-1, keepdims=True)
+
+    for b in range(4):
+        at = pl.ds(256 * b, 256)
+        n = 256 * (b + 1)
+        i = lax.broadcasted_iota(jnp.int32, (256, n), 0) + 256 * b
+        j = lax.broadcasted_iota(jnp.int32, (256, n), 1)
+        same = (col_of(cols, 2 * b, 2 * b + 2) == row_of(rows, 0, 2 * b + 2)) & (i >= j)
+        ds = nt(r_scr[at, :], v[0:n, :]) - jnp.sum(m_scr[at, :], axis=-1, keepdims=True)
+        ds = jnp.where(same, ds, 0.0).astype(bf16)
+        qg = feature_back(phq[at, :], nn(ds, phk[0:n, :]), qk[at, 0:64])
+        m = 1024 - 256 * b
+        later = pl.ds(256 * b, m)
+        j2 = lax.broadcasted_iota(jnp.int32, (256, m), 0)
+        i2 = lax.broadcasted_iota(jnp.int32, (256, m), 1)
+        same2 = (col_of(cols, 2 * b, 2 * b + 2) == row_of(rows, 2 * b, 8)) & (i2 >= j2)
+        scores = jnp.where(same2, nt(phk[at, :], phq[later, :]), 0.0).astype(bf16)
+        vg = nn(scores, r_scr[later, :])
+        mr = nt(ones, m_scr[later, :], lax.Precision.HIGHEST)[0:1, :]
+        ds2 = jnp.where(same2, nt(v[at, :], r_scr[later, :]) - mr, 0.0).astype(bf16)
+        kg = feature_back(phk[at, :], nn(ds2, phq[later, :]), qk[at, 64:128])
+        rnd = lambda t: t.astype(bf16).astype(f32)
+        pg_o[at, :] = rnd(jnp.concatenate([qg, kg], axis=1))
+        pg_o[pl.ds(1024 + 256 * (b % 2), 256), 64 * (b // 2) : 64 * (b // 2) + 64] = rnd(vg)
+
+
+def weight_part(ids, mine, theirs, nt_low, q0, q1, q2, q3, keep, give, scr, g_scr):
+    z, c, first = ids[0], ids[1], ids[2]
+    for b in range(4):
+        at = pl.ds(256 * b, 256)
+        va = pl.ds(1024 + 256 * (b % 2), 256)
+        lanes = slice(64 * (b // 2), 64 * (b // 2) + 64)
+        a, t = mine[at, :], theirs[at, :]
+        av, tv = mine[va, lanes], theirs[va, lanes]
+        h0 = jnp.where(c == 0, a, t)
+        h1 = jnp.where(c == 0, t, a)
+        scr[at, 0:128] = jnp.concatenate([h0[:, 0:64], h1[:, 0:64]], axis=1)
+        scr[at, 128:256] = jnp.concatenate([h0[:, 64:128], h1[:, 64:128]], axis=1)
+        scr[at, 256:384] = jnp.concatenate([jnp.where(c == 0, av, tv), jnp.where(c == 0, tv, av)], axis=1)
+    for k, ref in enumerate((q0, q1, q2, q3)):
+        chunk = 2 * jnp.bitwise_xor(z, k) + c
+        ref[...] = scr[pl.ds(pl.multiple_of(chunk * 128, 128), 128), :]
+    g_scr[...] = nn(nt_low[...], scr[...].astype(bf16))
+    keep[...] = g_scr[pl.ds(pl.multiple_of(first * 128, 128), 128), :]
+    give[...] = g_scr[pl.ds(pl.multiple_of((1 - first) * 128, 128), 128), :]
+
+
+def tokens_part(ids, q0, q1, q2, q3, mg, tokens, w, gain, out_o, scr):
+    z = ids[0]
+    for k, ref in enumerate((q0, q1, q2, q3)):
+        j = jnp.bitwise_xor(z, k)
+        for part in range(3):
+            scr[:, pl.ds(pl.multiple_of(part * 512 + j * 128, 128), 128)] = ref[:, 128 * part : 128 * part + 128].astype(bf16)
+    n, inv = normalise(tokens[...].astype(f32))
+    e = gain[...] * nt(scr[...], w[...])
+    out_o[...] = mg[...] + normalise_back(e, n, inv)
+
+
+def add_split(ids, mine, got, keep, give):
+    second = ids[3]
+    a = pl.ds(pl.multiple_of(second * 64, 64), 64)
+    b = pl.ds(pl.multiple_of((1 - second) * 64, 64), 64)
+    keep[...] = mine[a, :] + got[a, :]
+    give[...] = mine[b, :] + got[b, :]
+
+
+def ffn_weights(count, first, last, ids, *refs):
+    xs, cs = refs[:count], refs[count : 2 * count]
+    wut, wd = refs[2 * count : 2 * count + 2]
+    rest = refs[2 * count + 2 :]
+    if not first:
+        up_in, down_in, rest = rest[0], rest[1], rest[2:]
+    if last:
+        up_o, down_o, gain_o, xb, cb = rest
+    else:
+        up_o, down_o, xb, cb = rest
+    step = pl.program_id(0)
+
+    @pl.when(step == 0)
+    def _():
+        at = 0
+        for x, cc in zip(xs, cs):
+            for i in range(x.shape[0]):
+                xb[pl.ds(at, 128), :] = x[i].astype(bf16)
+                cb[pl.ds(at, 128), :] = cc[i].astype(bf16)
+                at += 128
+
+    total_up = None
+    size = 512
+    for blk in range(xb.shape[0] // size):
+        at = pl.ds(blk * size, size)
+        x, inc = xb[at, :], cb[at, :]
+        up = nt(wut[...], x)
+        hg = nt(wd[...], inc)
+        cdf, pdf = gelu_parts(up)
+        du = nn(((cdf + up * pdf) * hg).astype(bf16), x)
+        dd = nn((up * cdf).astype(bf16), inc)
+        total_up = du if total_up is None else total_up + du
+        total_down = dd if blk == 0 else total_down + dd
+    if not first:
+        total_up = total_up + up_in[...]
+        total_down = total_down + down_in[...]
+    if last:
+        total_up = total_up * (1.0 / 32)
+        up_o[...] = jnp.transpose(total_up)
+        down_o[...] = total_down * (1.0 / 32)
+        part = jnp.sum(total_up * wut[...].astype(f32), axis=0, keepdims=True)
+
+        @pl.when(step == 0)
+        def _():
+            gain_o[...] = jnp.zeros((8, 512), f32)
+
+        gain_o[0:1, :] = gain_o[0:1, :] + part
+    else:
+        up_o[...] = total_up
+        down_o[...] = total_down
+
+
+def ffn_call(ids, xs, cs, wut, wd, carried, last):
+    count, first = len(xs), carried is None
+    tokens = count * 256
+    pair = lambda v: pl.BlockSpec((2, 128, 512), lambda i, ids, at=v[1]: (at, 0, 0))
+    block = pl.BlockSpec((256, 512), lambda i, ids: (i, 0))
+    in_specs = [pair(v) for v in xs] + [pair(v) for v in cs] + [block, block]
+    args = [v[0] for v in xs] + [v[0] for v in cs] + [wut, wd]
+    if not first:
+        in_specs += [block, block]
+        args += list(carried)
+    out_specs, out_shapes = [block, block], [(1024, 512), (1024, 512)]
+    if last:
+        out_specs = [
+            pl.BlockSpec((512, 256), lambda i, ids: (0, i + 4 * ids[1])),
+            pl.BlockSpec((256, 512), lambda i, ids: (i + 4 * ids[1], 0)),
+            pl.BlockSpec((8, 512), lambda i, ids: (0, 0)),
+        ]
+        out_shapes = [(512, 2048), (2048, 512), (8, 512)]
+    return pl.pallas_call(
+        functools.partial(ffn_weights, count, first, last),
+        grid_spec=pltpu.PrefetchScalarGridSpec(
+            num_scalar_prefetch=1,
+            grid=(4,),
+            in_specs=in_specs,
+            out_specs=out_specs,
+            scratch_shapes=[pltpu.VMEM((tokens, 512), bf16), pltpu.VMEM((tokens, 512), bf16)],
+        ),
+        out_shape=[jax.ShapeDtypeStruct(shape, f32) for shape in out_shapes],
+        compiler_params=pltpu.CompilerParams(vmem_limit_bytes=ROOM),
+        name="ffn_weights",
+        cost_estimate=work(tokens / 100),
+    )(ids, *args)
+
+
+def put_half(ids, up_in, down_in, up_any, down_any, up_o, down_o):
+    up_o[...] = up_in[...]
+    down_o[...] = down_in[...]
+
+
+def put_halves(ids, up, down, up_full, down_full):
+    up_spec = pl.BlockSpec((512, 256), lambda i, ids: (0, i + 4 - 4 * ids[1]))
+    down_spec = pl.BlockSpec((256, 512), lambda i, ids: (i + 4 - 4 * ids[1], 0))
+    whole = pl.BlockSpec(memory_space=pl.ANY)
+    return pl.pallas_call(
+        put_half,
+        grid_spec=pltpu.PrefetchScalarGridSpec(
+            num_scalar_prefetch=1,
+            grid=(4,),
+            in_specs=[pl.BlockSpec((512, 256), lambda i, ids: (0, i)), pl.BlockSpec((256, 512), lambda i, ids: (i, 0)), whole, whole],
+            out_specs=[up_spec, down_spec],
+        ),
+        out_shape=[jax.ShapeDtypeStruct((512, 2048), f32), jax.ShapeDtypeStruct((2048, 512), f32)],
+        input_output_aliases={3: 0, 4: 1},
+        compiler_params=pltpu.CompilerParams(vmem_limit_bytes=ROOM),
+        name="put_halves",
+        cost_estimate=work(3),
+    )(ids, up, down, up_full, down_full)
+
+
+def gather_all(own, split):
+    z1, z2, z3 = (send(own, ALONG_Z[k]) for k in (1, 2, 3))
+    groups = []
+    for members in ([own, z1], [z2, z3]) if split else ([own, z1, z2, z3],):
+        base = jnp.stack(members)
+        two = jnp.concatenate([base, send(base, FIRST)])
+        other = send(two, SECOND)
+        groups.append([two, other, send(two, CORES), send(other, CORES)])
+    return groups
+
+
+def finish(ids, a, f, ca, cf, w, gain, qkv_o, out_o, gain_o, total):
+    z, c, first, second = ids[0], ids[1], ids[2], ids[3]
+    for core, ref, r1, r2, flip in ((c, a, first, second, 0), (c, f, first, second, 1), (1 - c, ca, second, first, 0), (1 - c, cf, second, first, 1)):
+        for n in range(2):
+            row = core * 256 + jnp.bitwise_xor(r1, flip) * 128 + jnp.bitwise_xor(r2, n) * 64
+            rows = pl.ds(pl.multiple_of(row, 64), 64)
+            for k in range(4):
+                j = jnp.bitwise_xor(z, k)
+                for part in range(3):
+                    at = pl.ds(pl.multiple_of(part * 512 + j * 128, 128), 128)
+                    qkv_o[rows, at] = ref[4 * n + k, :, 128 * part : 128 * part + 128]
+                out_o[rows, pl.ds(pl.multiple_of(j * 128, 128), 128)] = ref[4 * n + k, :, 384:512]
+    for r in range(4):
+        rows = pl.ds(128 * r, 128)
+        acc = jnp.zeros((128, 128), f32)
+        for j in range(12):
+            lanes = pl.ds(128 * j, 128)
+            acc = acc + w[rows, lanes].astype(f32) * qkv_o[rows, lanes]
+        lanes = pl.ds(128 * r, 128)
+        gain_o[0:1, lanes] = jnp.sum(jnp.transpose(acc), axis=0, keepdims=True) / gain[0:1, lanes]
+
+
+def local_fast(tokens, doc_start, norm1_gain, qkv_weight, out_weight, norm2_gain, up_weight, down_weight, omega, cotangent):
+    dp, seq = lax.axis_index("dp"), lax.axis_index("seq")
+    y, x, z, c = dp // 2, dp % 2, seq // 2, seq % 2
+    first = jnp.where(c == 0, x, y)
+    second = jnp.where(c == 0, y, x)
+    ids = jnp.stack([z, c, first, second]).astype(jnp.int32)
+    g1, g2 = norm1_gain.reshape(1, 512), norm2_gain.reshape(1, 512)
+    tok, cot = tokens[0], cotangent[0]
+    marks = jnp.pad(doc_start.astype(f32), ((0, 7), (0, 384)))
+    message = jnp.concatenate([tok.astype(f32), marks], axis=0)
+    t = [message] + [send(message, ALONG_Z[k]) for k in (1, 2, 3)]
+    p = [send(v, CORES) for v in t]
+    head = seq
+    wh = lax.dynamic_index_in_dim(qkv_weight.reshape(512, 3, 8, 64), head, 2, keepdims=False).reshape(512, 192)
+    om = lax.dynamic_index_in_dim(omega, head, 0, keepdims=False)
+    wut = jnp.transpose(lax.dynamic_slice_in_dim(up_weight, c * 1024, 1024, 1))
+    wdh = lax.dynamic_slice_in_dim(down_weight, c * 1024, 1024, 0)
+    keep, give, phq, phk, qk, v, mxd, doc, nt_low = kernel_call(
+        head_forward,
+        [((4, 128, 64), f32), ((4, 128, 64), f32), ((1024, 256), bf16), ((1024, 256), bf16), ((1024, 128), f32),
+         ((1024, 64), bf16), ((1024, 128), f32), ((8, 128), f32), ((256, 1024), bf16)],
+        ids, [*t, *p, g1, wh, om], [pltpu.VMEM((1024, 512), bf16)], "head_forward", 7,
+    )
+    block = ((128, 128), f32)
+    b = kernel_call(pack_pairs, [block] * 4, ids, [keep, send(give, CORES)], name="pack_pairs")
+    b = [b[0]] + [send(b[k], ALONG_Z[k]) for k in (1, 2, 3)]
+    mixed, middle, normed = kernel_call(
+        middle_part, [((128, 512), bf16), ((128, 512), f32), ((128, 512), f32)], ids, [*b, tok, out_weight, g2],
+        name="middle_part",
+    )
+    (cot_group,) = gather_all(cot.astype(f32), False)
+    x_groups = gather_all(normed, True)
+    output, mg, mlow, ex, *b = kernel_call(
+        feed_forward,
+        [((128, 512), bf16), ((128, 512), f32), ((128, 512), bf16), ((128, 768), f32)] + [block] * 4,
+        ids, [mixed, middle, normed, cot, up_weight, down_weight, out_weight, g2], [pltpu.VMEM((128, 512), f32)],
+        "feed_forward", 7,
+    )
+    b = [b[0]] + [send(b[k], ALONG_Z[k]) for k in (1, 2, 3)]
+    keep, give = kernel_call(unpack_pairs, [((4, 128, 64), f32)] * 2, ids, b, name="unpack_pairs")
+    got = send(give, CORES)
+    okeep, ogive = kernel_call(out_part, [((128, 512), f32)] * 2, ids, [mixed, mlow, send(ex, CORES)],
+                             [pltpu.VMEM((256, 512), f32)], "out_part")
+    okeep, ogive = kernel_call(add_split, [((64, 512), f32)] * 2, ids, [okeep, send(ogive, FIRST)], name="add_split")
+    o = kernel_call(add_spread, [((64, 128), f32)] * 4, ids, [okeep, send(ogive, SECOND)],
+                    [pltpu.VMEM((64, 512), f32)], "add_spread")
+    o = [o[0]] + [send(o[k], ALONG_Z[k]) for k in (1, 2, 3)]
+    (pg,) = kernel_call(
+        head_backward, [((1536, 128), f32)], ids, [keep, got, phq, phk, qk, v, mxd, doc, om],
+        [pltpu.VMEM((1024, 64), bf16), pltpu.VMEM((1024, 64), f32)], "head_backward", 9,
+    )
+    *q, keep, give = kernel_call(
+        weight_part, [((128, 384), f32)] * 4 + [((128, 384), f32)] * 2, ids, [pg, send(pg, CORES), nt_low],
+        [pltpu.VMEM((1024, 384), f32), pltpu.VMEM((256, 384), f32)], "weight_part",
+    )
+    keep, give = kernel_call(add_split, [((64, 384), f32)] * 2, ids, [keep, send(give, FIRST)], name="add_split")
+    (piece,) = kernel_call(add_last, [((64, 512), f32)], ids, [keep, send(give, SECOND), *o], name="add_last")
+    pieces = jnp.stack([piece] + [send(piece, ALONG_Z[k]) for k in (1, 2, 3)])
+    q = [q[0]] + [send(q[k], ALONG_Z[k]) for k in (1, 2, 3)]
+    (tokens_grad,) = kernel_call(
+        tokens_part, [((128, 512), f32)], ids, [*q, mg, tok, qkv_weight, g1], [pltpu.VMEM((128, 1536), bf16)],
+        "tokens_part",
+    )
+    carried = None
+    for i, xg in enumerate(x_groups):
+        xs = [(v, at) for v in xg for at in (0, 1)]
+        cs = [(v, at) for v in cot_group for at in (i, 2 + i)]
+        carried = ffn_call(ids, xs, cs, wut, wdh, carried, i == len(x_groups) - 1)
+    up_grad, down_grad, part2 = carried
+    up_half = lax.dynamic_slice_in_dim(up_grad, c * 1024, 1024, 1)
+    down_half = lax.dynamic_slice_in_dim(down_grad, c * 1024, 1024, 0)
+    up_grad, down_grad = put_halves(ids, send(up_half, CORES), send(down_half, CORES), up_grad, down_grad)
+    norm2_grad = (part2 + send(part2, CORES))[0] / norm2_gain
+    mine = jnp.concatenate([pieces, send(pieces, SECOND)])
+    theirs = send(mine, FIRST)
+    qkv_grad, out_grad, norm1_grad = kernel_call(
+        finish, [((512, 1536), f32), ((512, 512), f32), ((1, 512), f32)], ids,
+        [mine, theirs, send(mine, CORES), send(theirs, CORES), qkv_weight, g1], [pltpu.VMEM((8, 128), f32)], "finish", 5,
+    )
+    norm1_grad = norm1_grad[0]
+    return (output[None], tokens_grad[None], norm1_grad, qkv_grad, out_grad, norm2_grad, up_grad, down_grad)
+
+
 def solution(mesh):
     placed = (
         P("dp", "seq", None),
@@ -227,8 +775,9 @@
         P(),
         P("dp", "seq", None),
     )
+    fits = mesh.shape["dp"] == GRID_DP and mesh.shape["seq"] == GRID_SEQ
     return jax.shard_map(
-        local,
+        local_fast if fits else local,
         mesh=mesh,
         in_specs=placed,
         out_specs=(P("dp", "seq", None), P("dp", "seq", None), P(), P(), P(), P(), P(), P()),

time: 505 us -> 304 us (0.60)
  waiting for transfers between devices: 202 us -> 102 us
  Pallas kernels: 0 us -> 98.2 us
  blocking collectives: 89.1 us -> 0 us
  other arithmetic: 82.8 us -> 10.8 us
  starting transfers between devices: 0.12 us -> 62.2 us
  matrix products: 61.6 us -> 0 us
  local copies, waits for them, and re-layouts: 50.4 us -> 28.2 us
  between operations: 15.3 us -> 1.14 us
    psum x1 -> x0, waiting for transfers between devices: 185 us -> none  [local(): lax.psum((qkv_grad, out_grad, up_grad, down_grad, norm1_grad, norm2_grad)...]
    ppermute x0 -> x55, waiting for transfers between devices: none -> 102 us  [send(): return lax.ppermute(value, AXES, perm)]
    pallas_call x0 -> x17, Pallas kernels: none -> 98.2 us  [the longest x14 49.5 us: kernel_call(): pl.pallas_call(body, out_shape=[jax.ShapeDtypeStruct(s, d) for s, d in ou...]
    ppermute x0 -> x55, starting transfers between devices: none -> 62.2 us  [send(): return lax.ppermute(value, AXES, perm)]
    dot_general x30 -> x0, matrix products: 61.6 us -> none  [the longest x4 10.2 us: features(): jnp.einsum('...hd,hdm->...hm', scaled, omega, precision=highest_precision)]
    select_n x28 -> x0, other arithmetic: 53.1 us -> none  [hop(): jnp.where(position < mine, new, old)]
    psum x1 -> x0, blocking collectives: 40.8 us -> none  [local(): lax.psum((qkv_grad, out_grad, up_grad, down_grad, norm1_grad, norm2_grad)...]
    all_gather x2 -> x0, blocking collectives: 29.8 us -> none  [entering(): pieces = jax.tree.map(lambda part: lax.all_gather(part, axis), value)]
  transfers between devices with their start and end apart: 3 -> 55, of which waited for: 3 -> 19; matrix products, arithmetic and copies ran while one was open for 7% -> 8% of each run, Pallas kernels for 0% -> 31%
where the time goes in v1:
time: 304 us; the launch traced here: 303 us
  waiting for transfers between devices  102 us (34%)
  Pallas kernels  98.2 us (32%)
  starting transfers between devices  62.2 us (20%)
  local copies, waits for them, and re-layouts  28.2 us (9%)
  other arithmetic  10.8 us (4%)
    ppermute x55, waiting for transfers between devices, send(): return lax.ppermute(value, AXES, perm)  102 us
    ppermute x55, starting transfers between devices, send(): return lax.ppermute(value, AXES, perm)  62.2 us
    pallas_call x14, Pallas kernels, kernel_call(): pl.pallas_call(body, out_shape=[jax.ShapeDtypeStruct(s, d) for s, d in ou...  49.5 us
    pallas_call x2, Pallas kernels, ffn_call(): pl.pallas_call(functools.partial(ffn_weights, count, first, last), grid_s...  43.2 us
    unnamed x99, local copies, waits for them, and re-layouts  18.3 us
  transfers between devices with their start and end apart: 55, of which 19 were waited for; matrix products, arithmetic and copies ran while one was open for 8% of the time, Pallas kernels for 31%

profile of v1, /device:TPU:0, one launch (start us, length us, event | category | flops | bytes accessed | tf_op | source)
XLA Modules:
  0.0 302.9 jit_solution(17872881116403672212)
XLA Ops:
  0.6 1.8 fusion
  2.4 3.0 collective-permute-start.40
  7.8 3.0 collective-permute-start.1
  10.8 1.3 collective-permute-start.2
  12.2 1.7 collective-permute-start.41
  13.9 1.7 copy.22
  16.3 2.5 collective-permute-done.40
  18.8 3.5 %collective-permute-start.42 = (f32[128,512]{1,0:T(8,128)}, f32[128,512]{1,0:T(8,128)S(1)}, u32[]{:S(2)}, u32[]{:S(2)}) collective-permute-start(f32[128,512]{1,0:T(8,128)} %get-tuple-element.113), channel_id=1, source_target_pairs={{0,6},{1,7},{2,4},{3,5},{4,2},{5,3},{6,0},{7,1},{8,14},{9,15},{10,... | collective-permute-start | bytes 786440 | tf_op jit(solution)/shard_map/ppermute | solution.py:250
  22.3 31.1 %collective-permute-done.41 = f32[128,512]{1,0:T(8,128)S(1)} collective-permute-done((f32[128,512]{1,0:T(8,128)}, f32[128,512]{1,0:T(8,128)S(1)}, u32[]{:S(2)}, u32[]{:S(2)}) %collective-permute-start.41) | collective-permute-done | bytes 262176 | tf_op jit(solution)/shard_map/ppermute | solution.py:250
  56.6 1.9 collective-permute-start.43
  59.4 6.7 %head_forward.1 = (f32[4,128,64]{2,1,0:T(8,128)}, f32[4,128,64]{2,1,0:T(8,128)}, bf16[1024,256]{1,0:T(8,128)(2,1)}, bf16[1024,256]{1,0:T(8,128)(2,1)}, f32[1024,...) custom-call(s32[4]{0:T(128)} %pad_add_fusion.ids, ...), custom_call_target="tpu_custom_call" | custom-call | flops 7000000000 | tf_op jit(solution)/shard_map/head_forward/pallas_call | solution.py:271
  68.6 1.9 pack_pairs.1
  70.5 3.6 %collective-permute-start.10 = (f32[128,128]{1,0:T(8,128)}, f32[128,128]{1,0:T(8,128)S(1)}, u32[]{:S(2)}, u32[]{:S(2)}) collective-permute-start(f32[128,128]{1,0:T(8,128)} %get-tuple-element.65), channel_id=1, source_target_pairs={{0,6},{1,7},{2,4},{3,5},{4,2},{5,3},{6,0},{7,1},{8,14},{9,15},{10,... | collective-permute-start | bytes 196616 | tf_op jit(solution)/shard_map/ppermute | solution.py:250
  75.6 1.6 collective-permute-done.10.b3
  77.1 2.1 collective-permute-done.8.b1
  80.9 2.3 middle_part.1
  83.2 6.9 %feed_forward.1 = (bf16[128,512]{1,0:T(8,128)(2,1)}, f32[128,512]{1,0:T(8,128)}, bf16[128,512]{1,0:T(8,128)(2,1)}, f32[128,768]{1,0:T(8,128)}, f32[128,128]{1,0:...) custom-call(s32[4]{0:T(128)} %pad_add_fusion.ids, ...), custom_call_target="tpu_custom_call" | custom-call | flops 7000000000 | tf_op jit(solution)/shard_map/feed_forward/pallas_call | solution.py:271
  91.3 2.6 collective-permute-start.12
  95.1 3.4 %collective-permute-done.12.b2 = f32[128,128]{1,0:T(8,128)S(1)} collective-permute-done((f32[128,128]{1,0:T(8,128)}, f32[128,128]{1,0:T(8,128)S(1)}, u32[]{:S(2)}, u32[]{:S(2)}) %collective-permute-start.12) | collective-permute-done | bytes 65568 | tf_op jit(solution)/shard_map/ppermute | solution.py:250
  98.6 1.6 collective-permute-done.13.b3
  100.8 1.9 unpack_pairs.1
  103.8 1.5 collective-permute-start.44
  106.0 9.0 %head_backward.1.mine = f32[1536,128]{1,0:T(8,128)} custom-call(s32[4]{0:T(128)} %pad_add_fusion.ids, f32[4,128,64]{2,1,0:T(8,128)} %get-tuple-element.74.keep, f32[4,128,64]{2,1,0:T(8,128)} %copy-done.23, bf16[1024,256]{1,0:T(8,128)(2,1)} %get-tuple-element.76.phq, bf16[1024,256]{1,0:T(8,128)(2,1)} %get-tuple-element.77.phk, ...), custom_call_target="tpu_custom_call" | custom-call | flops 8999999488 | tf_op jit(solution)/shard_map/head_backward/pallas_call | solution.py:271
  115.9 2.2 out_part.1
  118.8 5.0 %collective-permute-done.47 = f32[128,512]{1,0:T(8,128)S(1)} collective-permute-done((f32[128,512]{1,0:T(8,128)S(1)}, f32[128,512]{1,0:T(8,128)S(1)}, u32[]{:S(2)}, u32[]{:S(2)}) %collective-permute-start.47) | collective-permute-done | bytes 262176 | tf_op jit(solution)/shard_map/ppermute | solution.py:250
  124.4 3.2 %collective-permute-done.22.got = f32[128,512]{1,0:T(8,128)S(1)} collective-permute-done((f32[128,512]{1,0:T(8,128)}, f32[128,512]{1,0:T(8,128)S(1)}, u32[]{:S(2)}, u32[]{:S(2)}) %collective-permute-start.22) | collective-permute-done | bytes 262176 | tf_op jit(solution)/shard_map/ppermute | solution.py:250
  128.3 1.8 add_split.3
  131.7 3.2 %weight_part.1 = (f32[128,384]{1,0:T(8,128)}, f32[128,384]{1,0:T(8,128)}, f32[128,384]{1,0:T(8,128)}, f32[128,384]{1,0:T(8,128)}, f32[128,384]{1,0:T(8,128)}, /*index=5*/f32[128,384]{1,0:T(8,128)}) custom-call(s32[4]{0:T(128)} %pad_add_fusion.ids, f32[1536,128]{1,0:T(8,128)} %head_backward.1.mine, f32[1536,128]{1,0:T(8,128)} %copy-done.17, ...), custom_call_target="tpu_custom_call" | custom-call | flops 2000000000 | tf_op jit(solution)/shard_map/weight_part/pallas_call | solution.py:271
  134.8 1.4 collective-permute-start.19
  136.3 2.1 collective-permute-start.34
  138.4 3.1 %collective-permute-done.23.got = f32[64,512]{1,0:T(8,128)S(1)} collective-permute-done((f32[64,512]{1,0:T(8,128)}, f32[64,512]{1,0:T(8,128)S(1)}, u32[]{:S(2)}, u32[]{:S(2)}) %collective-permute-start.23) | collective-permute-done | bytes 131104 | tf_op jit(solution)/shard_map/ppermute | solution.py:250
  142.1 1.6 add_spread.1
  144.9 1.7 add_split.2
  146.7 3.3 %collective-permute-start.26 = (f32[64,128]{1,0:T(8,128)S(1)}, f32[64,128]{1,0:T(8,128)S(1)}, u32[]{:S(2)}, u32[]{:S(2)}) collective-permute-start(f32[64,128]{1,0:T(8,128)S(1)} %copy-done.43), channel_id=1, source_target_pairs={{0,6},{1,7},{2,4},{3,5},{4,2},{5,3},{6,0},{7,1},{8,14},{9,15},{10,... | collective-permute-start | bytes 98312 | tf_op jit(solution)/shard_map/ppermute | solution.py:250
  150.0 2.0 collective-permute-start.20
  152.1 2.2 collective-permute-start.35
  155.8 1.7 add_last.1
  158.0 3.6 %collective-permute-done.35 = f32[128,512]{1,0:T(8,128)S(1)} collective-permute-done((f32[128,512]{1,0:T(8,128)S(1)}, f32[128,512]{1,0:T(8,128)S(1)}, u32[]{:S(2)}, u32[]{:S(2)}) %collective-permute-start.35) | collective-permute-done | bytes 262176 | tf_op jit(solution)/shard_map/ppermute | solution.py:250
  161.6 3.8 %collective-permute-start.28 = (f32[64,512]{1,0:T(8,128)}, f32[64,512]{1,0:T(8,128)S(1)}, u32[]{:S(2)}, u32[]{:S(2)}) collective-permute-start(f32[64,512]{1,0:T(8,128)} %add_last.1), channel_id=1, source_target_pairs={{0,4},{1,5},{2,6},{3,7},{4,0},{5,1},{6,2},{7,3},{8,12},{9,13},{10,... | collective-permute-start | bytes 393224 | tf_op jit(solution)/shard_map/ppermute | solution.py:250
  165.4 2.4 collective-permute-start.29
  168.6 5.6 %collective-permute-done.28 = f32[64,512]{1,0:T(8,128)S(1)} collective-permute-done((f32[64,512]{1,0:T(8,128)}, f32[64,512]{1,0:T(8,128)S(1)}, u32[]{:S(2)}, u32[]{:S(2)}) %collective-permute-start.28) | collective-permute-done | bytes 131104 | tf_op jit(solution)/shard_map/ppermute | solution.py:250
  174.3 1.9 collective-permute-start.36
  176.2 1.7 pad_maximum_fusion.3
  177.9 1.5 collective-permute-start.30
  179.4 1.4 constant_dynamic-slice_fusion.3
  180.8 6.0 %collective-permute-done.36 = f32[2,128,512]{2,1,0:T(8,128)} collective-permute-done((f32[2,128,512]{2,1,0:T(8,128)}, f32[2,128,512]{2,1,0:T(8,128)}, u32[]{:S(2)}, u32[]{:S(2)}) %collective-permute-start.36) | collective-permute-done | bytes 524320 | tf_op jit(solution)/shard_map/ppermute | solution.py:250
  186.8 2.1 pad_maximum_fusion.refs_0_.refs_1_
  188.9 1.5 collective-permute-start.37
  191.9 1.4 copy.25
  193.5 10.5 %collective-permute-done.37.refs_2_.refs_3_ = f32[4,128,512]{2,1,0:T(8,128)} collective-permute-done((f32[4,128,512]{2,1,0:T(8,128)}, f32[4,128,512]{2,1,0:T(8,128)}, u32[]{:S(2)}, u32[]{:S(2)}) %collective-permute-start.37) | collective-permute-done | bytes 1048608 | tf_op jit(solution)/shard_map/ppermute | solution.py:250
  204.0 1.7 collective-permute-start.31
  205.7 21.1 %ffn_weights.2 = (f32[1024,512]{1,0:T(8,128)}, f32[1024,512]{1,0:T(8,128)}) custom-call(s32[4]{0:T(128)} %pad_add_fusion.ids, f32[4,128,512]{2,1,0:T(8,128)} %copy-done.5, f32[4,128,512]{2,1,0:T(8,128)} %copy-done.5, f32[4,128,512]{2,1,0:T(8,128)} %collective-permute-done.49.refs_2_.refs_3_, f32[4,128,512]{2,1,0:T(8,128)} %collective-permute-done.49.refs_2_.refs_3_, ...), custom_call_target="tpu_custom_call" | custom-call | flops 20480000000 | tf_op jit(solution)/shard_map/ffn_weights/pallas_call | solution.py:608
  228.2 22.1 %ffn_weights.3 = (f32[512,2048]{1,0:T(8,128)}, f32[2048,512]{1,0:T(8,128)}, f32[8,512]{1,0:T(8,128)}) custom-call(s32[4]{0:T(128)} %pad_add_fusion.ids, f32[4,128,512]{2,1,0:T(8,128)} %pad_maximum_fusion.refs_0_.refs_1_, f32[4,128,512]{2,1,0:T(8,128)} %pad_maximum_fusion.refs_0_.refs_1_, f32[4,128,512]{2,1,0:T(8,128)} %collective-permute-done.37.refs_2_.refs_3_, ...), custom_call_target="tpu_custom_call" | custom-call | flops 20480000000 | tf_op jit(solution)/shard_map/ffn_weights/pallas_call | solution.py:608
  250.3 3.3 %constant_dynamic-slice_fusion.1 = f32[512,1024]{1,0:T(8,128)} fusion(f32[512,2048]{1,0:T(8,128)} %get-tuple-element.108.up_any, s32[]{:T(128)S(6)} %select_n.43), kind=kLoop, calls=%fused_computation.21 | loop fusion | bytes 4194308 | tf_op jit(solution)/shard_map/dynamic_slice | solution.py:751
  253.7 1.5 constant_dynamic-slice_fusion
  256.2 6.9 %collective-permute-done.16.q1 = f32[128,384]{1,0:T(8,128)S(1)} collective-permute-done((f32[128,384]{1,0:T(8,128)S(1)}, f32[128,384]{1,0:T(8,128)S(1)}, u32[]{:S(2)}, u32[]{:S(2)}) %collective-permute-start.16) | collective-permute-done | bytes 196640 | tf_op jit(solution)/shard_map/ppermute | solution.py:250
  263.1 2.9 collective-permute-start.17
  266.0 9.0 %collective-permute-done.17.q2 = f32[128,384]{1,0:T(8,128)S(1)} collective-permute-done((f32[128,384]{1,0:T(8,128)S(1)}, f32[128,384]{1,0:T(8,128)S(1)}, u32[]{:S(2)}, u32[]{:S(2)}) %collective-permute-start.17) | collective-permute-done | bytes 196640 | tf_op jit(solution)/shard_map/ppermute | solution.py:250
  275.0 3.5 %collective-permute-start.18 = (f32[128,384]{1,0:T(8,128)S(1)}, f32[128,384]{1,0:T(8,128)S(1)}, u32[]{:S(2)}, u32[]{:S(2)}) collective-permute-start(f32[128,384]{1,0:T(8,128)S(1)} %copy-done.26), channel_id=1, source_target_pairs={{0,6},{1,7},{2,4},{3,5},{4,2},{5,3},{6,0},{7,1},{8,14},{9,15},{10,... | collective-permute-start | bytes 589832 | tf_op jit(solution)/shard_map/ppermute | solution.py:250
  278.5 5.1 %collective-permute-done.18.q3 = f32[128,384]{1,0:T(8,128)S(1)} collective-permute-done((f32[128,384]{1,0:T(8,128)S(1)}, f32[128,384]{1,0:T(8,128)S(1)}, u32[]{:S(2)}, u32[]{:S(2)}) %collective-permute-start.18) | collective-permute-done | bytes 196640 | tf_op jit(solution)/shard_map/ppermute | solution.py:250
  284.4 3.4 %tokens_part.1 = f32[128,512]{1,0:T(8,128)} custom-call(s32[4]{0:T(128)} %pad_add_fusion.ids, f32[128,384]{1,0:T(8,128)} %get-tuple-element.83.q0, f32[128,384]{1,0:T(8,128)} %copy-done.30, f32[128,384]{1,0:T(8,128)} %copy-done.31, f32[128,384]{1,0:T(8,128)} %copy-done.32, f32[128,512]{1,0:T(8,128)} %get-tuple-element.87.mg, bf16[128,512]{1,0:T(8,128)(2,1)} %bitcast.58, ...), custom_call_target="tpu_custom_call" | custom-call | flops 2000000000 | tf_op jit(solution)/shard_map/tokens_part/pallas_call | solution.py:271
  288.9 5.2 %finish.1 = (f32[512,1536]{1,0:T(8,128)}, f32[512,512]{1,0:T(8,128)}, f32[1,512]{1,0:T(1,128)}) custom-call(s32[4]{0:T(128)} %pad_add_fusion.ids, f32[8,64,512]{2,1,0:T(8,128)} %copy-done.10, f32[8,64,512]{2,1,0:T(8,128)} %copy-done.13, f32[8,64,512]{2,1,0:T(8,128)} %copy-done.14, f32[8,64,512]{2,1,0:T(8,128)} %collective-permute-done.33.cf, ...), custom_call_target="tpu_custom_call" | custom-call | flops 5000000000 | tf_op jit(solution)/shard_map/finish/pallas_call | solution.py:271
  294.7 1.3 copy-done.3
  297.4 5.5 %put_halves.1 = (f32[512,2048]{1,0:T(8,128)}, f32[2048,512]{1,0:T(8,128)}) custom-call(s32[4]{0:T(128)} %pad_add_fusion.ids, f32[512,1024]{1,0:T(8,128)} %copy-done.3, f32[1024,512]{1,0:T(8,128)} %copy-done.4, f32[512,2048]{1,0:T(8,128)} %get-tuple-element.108.up_any, ...), custom_call_target="tpu_custom_call", output_to_operand_aliasing={{0}: (3, {}), {1}: (4, {})} | custom-call | flops 3000000000 | tf_op jit(solution)/shard_map/put_halves/pallas_call | solution.py:633
  (185 shorter events, 34.7 us)
Async XLA Ops:
  0.6 55.2 %copy-start = (f32[8,64,256]{2,1,0:T(8,128)S(1)}, f32[8,64,256]{2,1,0:T(8,128)}, u32[]{:S(2)}) copy-start(f32[8,64,256]{2,1,0:T(8,128)} %param.18) | copy-start | bytes 1572868
  2.4 13.1 %copy-start.7 = (bf16[1,128,512]{2,1,0:T(8,128)(2,1)S(1)}, bf16[1,128,512]{2,1,0:T(8,128)(2,1)}, u32[]{:S(2)}) copy-start(bf16[1,128,512]{2,1,0:T(8,128)(2,1)} %param.19) | copy-start | bytes 393220
  2.4 16.3 %collective-permute-start.40 = (f32[128,512]{1,0:T(8,128)}, f32[128,512]{1,0:T(8,128)S(1)}, u32[]{:S(2)}, u32[]{:S(2)}) collective-permute-start(f32[128,512]{1,0:T(8,128)} %get-tuple-element.113), channel_id=1, source_target_pairs={{0,2},{1,3},{2,0},{3,1},{4,6},{5,7},{6,4},{7,5},{8,10},{9,11},{10,... | collective-permute-start | bytes 786440 | tf_op jit(solution)/shard_map/ppermute | solution.py:250
  7.8 45.6 %collective-permute-start = (f32[136,512]{1,0:T(8,128)}, f32[136,512]{1,0:T(8,128)}, u32[]{:S(2)}, u32[]{:S(2)}) collective-permute-start(f32[136,512]{1,0:T(8,128)} %select_maximum_fusion.t0), channel_id=1, source_target_pairs={{0,2},{1,3},{2,0},{3,1},{4,6},{5,7},{6,4},{7,5},{8,10},{9,11},{10,... | collective-permute-start | bytes 835592 | tf_op jit(solution)/shard_map/ppermute | solution.py:250
  7.8 46.1 %collective-permute-start.1 = (f32[136,512]{1,0:T(8,128)}, f32[136,512]{1,0:T(8,128)}, u32[]{:S(2)}, u32[]{:S(2)}) collective-permute-start(f32[136,512]{1,0:T(8,128)} %select_maximum_fusion.t0), channel_id=1, source_target_pairs={{0,4},{1,5},{2,6},{3,7},{4,0},{5,1},{6,2},{7,3},{8,12},{9,13},{10,... | collective-permute-start | bytes 835592 | tf_op jit(solution)/shard_map/ppermute | solution.py:250
  10.8 43.2 %collective-permute-start.2 = (f32[136,512]{1,0:T(8,128)}, f32[136,512]{1,0:T(8,128)}, u32[]{:S(2)}, u32[]{:S(2)}) collective-permute-start(f32[136,512]{1,0:T(8,128)} %select_maximum_fusion.t0), channel_id=1, source_target_pairs={{0,6},{1,7},{2,4},{3,5},{4,2},{5,3},{6,0},{7,1},{8,14},{9,15},{10,... | collective-permute-start | bytes 835592 | tf_op jit(solution)/shard_map/ppermute | solution.py:250
  12.2 41.2 %collective-permute-start.41 = (f32[128,512]{1,0:T(8,128)}, f32[128,512]{1,0:T(8,128)S(1)}, u32[]{:S(2)}, u32[]{:S(2)}) collective-permute-start(f32[128,512]{1,0:T(8,128)} %get-tuple-element.113), channel_id=1, source_target_pairs={{0,4},{1,5},{2,6},{3,7},{4,0},{5,1},{6,2},{7,3},{8,12},{9,13},{10,... | collective-permute-start | bytes 786440 | tf_op jit(solution)/shard_map/ppermute | solution.py:250
  18.8 37.7 %collective-permute-start.42 = (f32[128,512]{1,0:T(8,128)}, f32[128,512]{1,0:T(8,128)S(1)}, u32[]{:S(2)}, u32[]{:S(2)}) collective-permute-start(f32[128,512]{1,0:T(8,128)} %get-tuple-element.113), channel_id=1, source_target_pairs={{0,6},{1,7},{2,4},{3,5},{4,2},{5,3},{6,0},{7,1},{8,14},{9,15},{10,... | collective-permute-start | bytes 786440 | tf_op jit(solution)/shard_map/ppermute | solution.py:250
  53.4 5.0 %collective-permute-start.3 = (f32[136,512]{1,0:T(8,128)}, f32[136,512]{1,0:T(8,128)S(1)}, u32[]{:S(2)}, u32[]{:S(2)}) collective-permute-start(f32[136,512]{1,0:T(8,128)} %select_maximum_fusion.t0), channel_id=1, source_target_pairs={{0,1},{1,0},{2,3},{3,2},{4,5},{5,4},{6,7},{7,6},{8,9},{9,8},{10,11... | collective-permute-start | bytes 835592 | tf_op jit(solution)/shard_map/ppermute | solution.py:250
  53.4 5.0 %collective-permute-start.4 = (f32[136,512]{1,0:T(8,128)}, f32[136,512]{1,0:T(8,128)S(1)}, u32[]{:S(2)}, u32[]{:S(2)}) collective-permute-start(f32[136,512]{1,0:T(8,128)} %collective-permute-done.t1), channel_id=1, source_target_pairs={{0,1},{1,0},{2,3},{3,2},{4,5},{5,4},{6,7},{7,6},{8,9},{9,8},{10,11... | collective-permute-start | bytes 835592 | tf_op jit(solution)/shard_map/ppermute | solution.py:250
  53.9 4.6 %collective-permute-start.5 = (f32[136,512]{1,0:T(8,128)}, f32[136,512]{1,0:T(8,128)S(1)}, u32[]{:S(2)}, u32[]{:S(2)}) collective-permute-start(f32[136,512]{1,0:T(8,128)} %collective-permute-done.1.t2), channel_id=1, source_target_pairs={{0,1},{1,0},{2,3},{3,2},{4,5},{5,4},{6,7},{7,6},{8,9},{9,8},{10,11... | collective-permute-start | bytes 835592 | tf_op jit(solution)/shard_map/ppermute | solution.py:250
  54.0 4.5 %collective-permute-start.6 = (f32[136,512]{1,0:T(8,128)}, f32[136,512]{1,0:T(8,128)S(1)}, u32[]{:S(2)}, u32[]{:S(2)}) collective-permute-start(f32[136,512]{1,0:T(8,128)} %collective-permute-done.2.t3), channel_id=1, source_target_pairs={{0,1},{1,0},{2,3},{3,2},{4,5},{5,4},{6,7},{7,6},{8,9},{9,8},{10,11... | collective-permute-start | bytes 835592 | tf_op jit(solution)/shard_map/ppermute | solution.py:250
  56.6 46.2 %collective-permute-start.43 = (f32[4,128,512]{2,1,0:T(8,128)S(1)}, f32[4,128,512]{2,1,0:T(8,128)S(1)}, u32[]{:S(2)}, u32[]{:S(2)}) collective-permute-start(f32[4,128,512]{2,1,0:T(8,128)S(1)} %pad_maximum_fusion.1), channel_id=1, source_target_pairs={{0,8},{1,17},{2,10},{3,19},{4,12},{5,21},{6,14},{7,23},{8,0},{9,25... | collective-permute-start | bytes 3145736 | tf_op jit(solution)/shard_map/ppermute | solution.py:250
  66.1 1.7 collective-permute-start.7
  70.5 6.7 %collective-permute-start.10 = (f32[128,128]{1,0:T(8,128)}, f32[128,128]{1,0:T(8,128)S(1)}, u32[]{:S(2)}, u32[]{:S(2)}) collective-permute-start(f32[128,128]{1,0:T(8,128)} %get-tuple-element.65), channel_id=1, source_target_pairs={{0,6},{1,7},{2,4},{3,5},{4,2},{5,3},{6,0},{7,1},{8,14},{9,15},{10,... | collective-permute-start | bytes 196616 | tf_op jit(solution)/shard_map/ppermute | solution.py:250
  74.1 5.2 %collective-permute-start.8 = (f32[128,128]{1,0:T(8,128)}, f32[128,128]{1,0:T(8,128)S(1)}, u32[]{:S(2)}, u32[]{:S(2)}) collective-permute-start(f32[128,128]{1,0:T(8,128)} %get-tuple-element.63), channel_id=1, source_target_pairs={{0,2},{1,3},{2,0},{3,1},{4,6},{5,7},{6,4},{7,5},{8,10},{9,11},{10,... | collective-permute-start | bytes 196616 | tf_op jit(solution)/shard_map/ppermute | solution.py:250
  74.5 5.7 %collective-permute-start.9 = (f32[128,128]{1,0:T(8,128)}, f32[128,128]{1,0:T(8,128)S(1)}, u32[]{:S(2)}, u32[]{:S(2)}) collective-permute-start(f32[128,128]{1,0:T(8,128)} %get-tuple-element.64), channel_id=1, source_target_pairs={{0,4},{1,5},{2,6},{3,7},{4,0},{5,1},{6,2},{7,3},{8,12},{9,13},{10,... | collective-permute-start | bytes 196616 | tf_op jit(solution)/shard_map/ppermute | solution.py:250
  90.0 5.1 %collective-permute-start.11 = (f32[128,128]{1,0:T(8,128)}, f32[128,128]{1,0:T(8,128)S(1)}, u32[]{:S(2)}, u32[]{:S(2)}) collective-permute-start(f32[128,128]{1,0:T(8,128)} %get-tuple-element.71), channel_id=1, source_target_pairs={{0,2},{1,3},{2,0},{3,1},{4,6},{5,7},{6,4},{7,5},{8,10},{9,11},{10,... | collective-permute-start | bytes 196616 | tf_op jit(solution)/shard_map/ppermute | solution.py:250
  91.3 7.3 %collective-permute-start.12 = (f32[128,128]{1,0:T(8,128)}, f32[128,128]{1,0:T(8,128)S(1)}, u32[]{:S(2)}, u32[]{:S(2)}) collective-permute-start(f32[128,128]{1,0:T(8,128)} %get-tuple-element.72), channel_id=1, source_target_pairs={{0,4},{1,5},{2,6},{3,7},{4,0},{5,1},{6,2},{7,3},{8,12},{9,13},{10,... | collective-permute-start | bytes 196616 | tf_op jit(solution)/shard_map/ppermute | solution.py:250
  93.9 6.3 %collective-permute-start.13 = (f32[128,128]{1,0:T(8,128)}, f32[128,128]{1,0:T(8,128)S(1)}, u32[]{:S(2)}, u32[]{:S(2)}) collective-permute-start(f32[128,128]{1,0:T(8,128)} %get-tuple-element.73), channel_id=1, source_target_pairs={{0,6},{1,7},{2,4},{3,5},{4,2},{5,3},{6,0},{7,1},{8,14},{9,15},{10,... | collective-permute-start | bytes 196616 | tf_op jit(solution)/shard_map/ppermute | solution.py:250
  95.1 20.0 %collective-permute-start.21 = (f32[128,768]{1,0:T(8,128)}, f32[128,768]{1,0:T(8,128)S(1)}, u32[]{:S(2)}, u32[]{:S(2)}) collective-permute-start(f32[128,768]{1,0:T(8,128)} %get-tuple-element.93), channel_id=1, source_target_pairs={{0,1},{1,0},{2,3},{3,2},{4,5},{5,4},{6,7},{7,6},{8,9},{9,8},{10,11... | collective-permute-start | bytes 1179656 | tf_op jit(solution)/shard_map/ppermute | solution.py:250
  102.7 2.6 collective-permute-start.14
  103.8 53.7 %collective-permute-start.44 = (f32[8,128,512]{2,1,0:T(8,128)}, f32[8,128,512]{2,1,0:T(8,128)}, u32[]{:S(2)}, u32[]{:S(2)}) collective-permute-start(f32[8,128,512]{2,1,0:T(8,128)} %constant_dynamic-update-slice_fusion.5.refs_8_.refs_9_), channel_id=1, source_target_pairs={{0,16},{1,9},{2,18},{3,11},{4,20},{5,13},{6,22},{7,15},{8,24},{9,1... | collective-permute-start | bytes 6291464 | tf_op jit(solution)/shard_map/ppermute | solution.py:250
  115.0 15.8 %collective-permute-start.15 = (f32[1536,128]{1,0:T(8,128)}, f32[1536,128]{1,0:T(8,128)S(1)}, u32[]{:S(2)}, u32[]{:S(2)}) collective-permute-start(f32[1536,128]{1,0:T(8,128)} %head_backward.1.mine), channel_id=1, source_target_pairs={{0,1},{1,0},{2,3},{3,2},{4,5},{5,4},{6,7},{7,6},{8,9},{9,8},{10,11... | collective-permute-start | bytes 2359304 | tf_op jit(solution)/shard_map/ppermute | solution.py:250
  115.1 8.7 %collective-permute-start.47 = (f32[128,512]{1,0:T(8,128)S(1)}, f32[128,512]{1,0:T(8,128)S(1)}, u32[]{:S(2)}, u32[]{:S(2)}) collective-permute-start(f32[128,512]{1,0:T(8,128)S(1)} %copy-done.6), channel_id=1, source_target_pairs={{0,2},{1,3},{2,0},{3,1},{4,6},{5,7},{6,4},{7,5},{8,10},{9,11},{10,... | collective-permute-start | bytes 786440 | tf_op jit(solution)/shard_map/ppermute | solution.py:250
  118.1 9.5 %collective-permute-start.22 = (f32[128,512]{1,0:T(8,128)}, f32[128,512]{1,0:T(8,128)S(1)}, u32[]{:S(2)}, u32[]{:S(2)}) collective-permute-start(f32[128,512]{1,0:T(8,128)} %get-tuple-element.95), channel_id=1, source_target_pairs={{0,8},{1,17},{2,10},{3,19},{4,12},{5,21},{6,14},{7,23},{8,0},{9,25... | collective-permute-start | bytes 786440 | tf_op jit(solution)/shard_map/ppermute | solution.py:250
  123.8 22.9 %collective-permute-start.48 = (f32[2,128,512]{2,1,0:T(8,128)S(1)}, f32[2,128,512]{2,1,0:T(8,128)S(1)}, u32[]{:S(2)}, u32[]{:S(2)}) collective-permute-start(f32[2,128,512]{2,1,0:T(8,128)S(1)} %pad_maximum_fusion.5), channel_id=1, source_target_pairs={{0,8},{1,17},{2,10},{3,19},{4,12},{5,21},{6,14},{7,23},{8,0},{9,25... | collective-permute-start | bytes 1572872 | tf_op jit(solution)/shard_map/ppermute | solution.py:250
  130.1 11.4 %collective-permute-start.23 = (f32[64,512]{1,0:T(8,128)}, f32[64,512]{1,0:T(8,128)S(1)}, u32[]{:S(2)}, u32[]{:S(2)}) collective-permute-start(f32[64,512]{1,0:T(8,128)} %get-tuple-element.97), channel_id=1, source_target_pairs={{0,16},{1,9},{2,18},{3,11},{4,20},{5,13},{6,22},{7,15},{8,24},{9,1... | collective-permute-start | bytes 393224 | tf_op jit(solution)/shard_map/ppermute | solution.py:250
  134.8 8.9 %collective-permute-start.19 = (f32[128,384]{1,0:T(8,128)}, f32[128,384]{1,0:T(8,128)S(1)}, u32[]{:S(2)}, u32[]{:S(2)}) collective-permute-start(f32[128,384]{1,0:T(8,128)} %get-tuple-element.89), channel_id=1, source_target_pairs={{0,8},{1,17},{2,10},{3,19},{4,12},{5,21},{6,14},{7,23},{8,0},{9,25... | collective-permute-start | bytes 589832 | tf_op jit(solution)/shard_map/ppermute | solution.py:250
  136.3 21.2 %collective-permute-start.34 = (f32[128,512]{1,0:T(8,128)S(1)}, f32[128,512]{1,0:T(8,128)S(1)}, u32[]{:S(2)}, u32[]{:S(2)}) collective-permute-start(f32[128,512]{1,0:T(8,128)S(1)} %copy-done.6), channel_id=1, source_target_pairs={{0,4},{1,5},{2,6},{3,7},{4,0},{5,1},{6,2},{7,3},{8,12},{9,13},{10,... | collective-permute-start | bytes 786440 | tf_op jit(solution)/shard_map/ppermute | solution.py:250
  143.8 6.3 %collective-permute-start.24 = (f32[64,128]{1,0:T(8,128)}, f32[64,128]{1,0:T(8,128)S(1)}, u32[]{:S(2)}, u32[]{:S(2)}) collective-permute-start(f32[64,128]{1,0:T(8,128)} %get-tuple-element.99), channel_id=1, source_target_pairs={{0,2},{1,3},{2,0},{3,1},{4,6},{5,7},{6,4},{7,5},{8,10},{9,11},{10,... | collective-permute-start | bytes 98312 | tf_op jit(solution)/shard_map/ppermute | solution.py:250
  143.8 8.3 %collective-permute-start.25 = (f32[64,128]{1,0:T(8,128)}, f32[64,128]{1,0:T(8,128)S(1)}, u32[]{:S(2)}, u32[]{:S(2)}) collective-permute-start(f32[64,128]{1,0:T(8,128)} %get-tuple-element.100), channel_id=1, source_target_pairs={{0,4},{1,5},{2,6},{3,7},{4,0},{5,1},{6,2},{7,3},{8,12},{9,13},{10,... | collective-permute-start | bytes 98312 | tf_op jit(solution)/shard_map/ppermute | solution.py:250
  146.7 7.7 %collective-permute-start.26 = (f32[64,128]{1,0:T(8,128)S(1)}, f32[64,128]{1,0:T(8,128)S(1)}, u32[]{:S(2)}, u32[]{:S(2)}) collective-permute-start(f32[64,128]{1,0:T(8,128)S(1)} %copy-done.43), channel_id=1, source_target_pairs={{0,6},{1,7},{2,4},{3,5},{4,2},{5,3},{6,0},{7,1},{8,14},{9,15},{10,... | collective-permute-start | bytes 98312 | tf_op jit(solution)/shard_map/ppermute | solution.py:250
  150.0 5.1 %collective-permute-start.20 = (f32[64,384]{1,0:T(8,128)}, f32[64,384]{1,0:T(8,128)S(1)}, u32[]{:S(2)}, u32[]{:S(2)}) collective-permute-start(f32[64,384]{1,0:T(8,128)} %get-tuple-element.91), channel_id=1, source_target_pairs={{0,16},{1,9},{2,18},{3,11},{4,20},{5,13},{6,22},{7,15},{8,24},{9,1... | collective-permute-start | bytes 294920 | tf_op jit(solution)/shard_map/ppermute | solution.py:250
  152.1 34.7 %copy-start.5 = (f32[4,128,512]{2,1,0:T(8,128)}, f32[4,128,512]{2,1,0:T(8,128)S(1)}, u32[]{:S(2)}) copy-start(f32[4,128,512]{2,1,0:T(8,128)S(1)} %pad_maximum_fusion.2.refs_0_.refs_1_) | copy-start | bytes 3145732
  152.1 9.5 %collective-permute-start.35 = (f32[128,512]{1,0:T(8,128)S(1)}, f32[128,512]{1,0:T(8,128)S(1)}, u32[]{:S(2)}, u32[]{:S(2)}) collective-permute-start(f32[128,512]{1,0:T(8,128)S(1)} %copy-done.6), channel_id=1, source_target_pairs={{0,6},{1,7},{2,4},{3,5},{4,2},{5,3},{6,0},{7,1},{8,14},{9,15},{10,... | collective-permute-start | bytes 786440 | tf_op jit(solution)/shard_map/ppermute | solution.py:250
  154.4 34.5 %collective-permute-start.49 = (f32[4,128,512]{2,1,0:T(8,128)S(1)}, f32[4,128,512]{2,1,0:T(8,128)}, u32[]{:S(2)}, u32[]{:S(2)}) collective-permute-start(f32[4,128,512]{2,1,0:T(8,128)S(1)} %pad_maximum_fusion.2.refs_0_.refs_1_), channel_id=1, source_target_pairs={{0,16},{1,9},{2,18},{3,11},{4,20},{5,13},{6,22},{7,15},{8,24},{9,1... | collective-permute-start | bytes 3145736 | tf_op jit(solution)/shard_map/ppermute | solution.py:250
  157.4 8.0 %collective-permute-start.27 = (f32[64,512]{1,0:T(8,128)}, f32[64,512]{1,0:T(8,128)S(1)}, u32[]{:S(2)}, u32[]{:S(2)}) collective-permute-start(f32[64,512]{1,0:T(8,128)} %add_last.1), channel_id=1, source_target_pairs={{0,2},{1,3},{2,0},{3,1},{4,6},{5,7},{6,4},{7,5},{8,10},{9,11},{10,... | collective-permute-start | bytes 393224 | tf_op jit(solution)/shard_map/ppermute | solution.py:250
  157.5 46.5 %collective-permute-start.45 = (f32[8,128,512]{2,1,0:T(8,128)}, f32[8,128,512]{2,1,0:T(8,128)}, u32[]{:S(2)}, u32[]{:S(2)}) collective-permute-start(f32[8,128,512]{2,1,0:T(8,128)} %constant_dynamic-update-slice_fusion.5.refs_8_.refs_9_), channel_id=1, source_target_pairs={{0,1},{1,0},{2,3},{3,2},{4,5},{5,4},{6,7},{7,6},{8,9},{9,8},{10,11... | collective-permute-start | bytes 6291464 | tf_op jit(solution)/shard_map/ppermute | solution.py:250
  157.5 48.2 %collective-permute-start.46 = (f32[8,128,512]{2,1,0:T(8,128)}, f32[8,128,512]{2,1,0:T(8,128)}, u32[]{:S(2)}, u32[]{:S(2)}) collective-permute-start(f32[8,128,512]{2,1,0:T(8,128)} %collective-permute-done.44.refs_10_.refs_11_), channel_id=1, source_target_pairs={{0,1},{1,0},{2,3},{3,2},{4,5},{5,4},{6,7},{7,6},{8,9},{9,8},{10,11... | collective-permute-start | bytes 6291464 | tf_op jit(solution)/shard_map/ppermute | solution.py:250
  161.6 12.7 %collective-permute-start.28 = (f32[64,512]{1,0:T(8,128)}, f32[64,512]{1,0:T(8,128)S(1)}, u32[]{:S(2)}, u32[]{:S(2)}) collective-permute-start(f32[64,512]{1,0:T(8,128)} %add_last.1), channel_id=1, source_target_pairs={{0,4},{1,5},{2,6},{3,7},{4,0},{5,1},{6,2},{7,3},{8,12},{9,13},{10,... | collective-permute-start | bytes 393224 | tf_op jit(solution)/shard_map/ppermute | solution.py:250
  165.4 10.7 %collective-permute-start.29 = (f32[64,512]{1,0:T(8,128)}, f32[64,512]{1,0:T(8,128)S(1)}, u32[]{:S(2)}, u32[]{:S(2)}) collective-permute-start(f32[64,512]{1,0:T(8,128)} %add_last.1), channel_id=1, source_target_pairs={{0,6},{1,7},{2,4},{3,5},{4,2},{5,3},{6,0},{7,1},{8,14},{9,15},{10,... | collective-permute-start | bytes 393224 | tf_op jit(solution)/shard_map/ppermute | solution.py:250
  174.3 12.5 %collective-permute-start.36 = (f32[2,128,512]{2,1,0:T(8,128)}, f32[2,128,512]{2,1,0:T(8,128)}, u32[]{:S(2)}, u32[]{:S(2)}) collective-permute-start(f32[2,128,512]{2,1,0:T(8,128)} %pad_maximum_fusion.4), channel_id=1, source_target_pairs={{0,8},{1,17},{2,10},{3,19},{4,12},{5,21},{6,14},{7,23},{8,0},{9,25... | collective-permute-start | bytes 1572872 | tf_op jit(solution)/shard_map/ppermute | solution.py:250
  177.9 12.4 %collective-permute-start.30 = (f32[4,64,512]{2,1,0:T(8,128)}, f32[4,64,512]{2,1,0:T(8,128)S(1)}, u32[]{:S(2)}, u32[]{:S(2)}) collective-permute-start(f32[4,64,512]{2,1,0:T(8,128)} %pad_maximum_fusion.3), channel_id=1, source_target_pairs={{0,16},{1,9},{2,18},{3,11},{4,20},{5,13},{6,22},{7,15},{8,24},{9,1... | collective-permute-start | bytes 1572872 | tf_op jit(solution)/shard_map/ppermute | solution.py:250
  179.4 11.5 %copy-start.8 = (bf16[2048,512]{1,0:T(8,128)(2,1)S(1)}, bf16[2048,512]{1,0:T(8,128)(2,1)}, u32[]{:S(2)}) copy-start(bf16[2048,512]{1,0:T(8,128)(2,1)} %wd.1) | copy-start | bytes 6291460
  186.8 6.6 %collective-permute-start.50 = (f32[4,128,512]{2,1,0:T(8,128)S(1)}, f32[4,128,512]{2,1,0:T(8,128)}, u32[]{:S(2)}, u32[]{:S(2)}) collective-permute-start(f32[4,128,512]{2,1,0:T(8,128)S(1)} %pad_maximum_fusion.2.refs_0_.refs_1_), channel_id=1, source_target_pairs={{0,1},{1,0},{2,3},{3,2},{4,5},{5,4},{6,7},{7,6},{8,9},{9,8},{10,11... | collective-permute-start | bytes 3145736 | tf_op jit(solution)/shard_map/ppermute | solution.py:250
  188.9 15.1 %collective-permute-start.37 = (f32[4,128,512]{2,1,0:T(8,128)}, f32[4,128,512]{2,1,0:T(8,128)}, u32[]{:S(2)}, u32[]{:S(2)}) collective-permute-start(f32[4,128,512]{2,1,0:T(8,128)} %pad_maximum_fusion.refs_0_.refs_1_), channel_id=1, source_target_pairs={{0,16},{1,9},{2,18},{3,11},{4,20},{5,13},{6,22},{7,15},{8,24},{9,1... | collective-permute-start | bytes 3145736 | tf_op jit(solution)/shard_map/ppermute | solution.py:250
  190.3 15.4 %collective-permute-start.51 = (f32[4,128,512]{2,1,0:T(8,128)}, f32[4,128,512]{2,1,0:T(8,128)}, u32[]{:S(2)}, u32[]{:S(2)}) collective-permute-start(f32[4,128,512]{2,1,0:T(8,128)} %collective-permute-done.49.refs_2_.refs_3_), channel_id=1, source_target_pairs={{0,1},{1,0},{2,3},{3,2},{4,5},{5,4},{6,7},{7,6},{8,9},{9,8},{10,11... | collective-permute-start | bytes 3145736 | tf_op jit(solution)/shard_map/ppermute | solution.py:250
  193.4 62.3 %copy-start.10 = (f32[8,64,512]{2,1,0:T(8,128)}, f32[8,64,512]{2,1,0:T(8,128)S(1)}, u32[]{:S(2)}) copy-start(f32[8,64,512]{2,1,0:T(8,128)S(1)} %constant_dynamic-update-slice_fusion.a) | copy-start | bytes 3145732
  193.4 33.5 %collective-permute-start.38 = (f32[4,128,512]{2,1,0:T(8,128)}, f32[4,128,512]{2,1,0:T(8,128)S(1)}, u32[]{:S(2)}, u32[]{:S(2)}) collective-permute-start(f32[4,128,512]{2,1,0:T(8,128)} %pad_maximum_fusion.refs_0_.refs_1_), channel_id=1, source_target_pairs={{0,1},{1,0},{2,3},{3,2},{4,5},{5,4},{6,7},{7,6},{8,9},{9,8},{10,11... | collective-permute-start | bytes 3145736 | tf_op jit(solution)/shard_map/ppermute | solution.py:250
  204.0 22.9 %collective-permute-start.39 = (f32[4,128,512]{2,1,0:T(8,128)}, f32[4,128,512]{2,1,0:T(8,128)S(1)}, u32[]{:S(2)}, u32[]{:S(2)}) collective-permute-start(f32[4,128,512]{2,1,0:T(8,128)} %collective-permute-done.37.refs_2_.refs_3_), channel_id=1, source_target_pairs={{0,1},{1,0},{2,3},{3,2},{4,5},{5,4},{6,7},{7,6},{8,9},{9,8},{10,11... | collective-permute-start | bytes 3145736 | tf_op jit(solution)/shard_map/ppermute | solution.py:250
  204.0 51.7 %collective-permute-start.31 = (f32[8,64,512]{2,1,0:T(8,128)S(1)}, f32[8,64,512]{2,1,0:T(8,128)S(1)}, u32[]{:S(2)}, u32[]{:S(2)}) collective-permute-start(f32[8,64,512]{2,1,0:T(8,128)S(1)} %constant_dynamic-update-slice_fusion.a), channel_id=1, source_target_pairs={{0,8},{1,17},{2,10},{3,19},{4,12},{5,21},{6,14},{7,23},{8,0},{9,25... | collective-permute-start | bytes 3145736 | tf_op jit(solution)/shard_map/ppermute | solution.py:250
  253.7 41.1 %collective-permute-start.53 = (f32[512,1024]{1,0:T(8,128)}, f32[512,1024]{1,0:T(8,128)S(1)}, u32[]{:S(2)}, u32[]{:S(2)}) collective-permute-start(f32[512,1024]{1,0:T(8,128)} %constant_dynamic-slice_fusion.1), channel_id=1, source_target_pairs={{0,1},{1,0},{2,3},{3,2},{4,5},{5,4},{6,7},{7,6},{8,9},{9,8},{10,11... | collective-permute-start | bytes 6291464 | tf_op jit(solution)/shard_map/ppermute | solution.py:250
  253.7 9.4 %copy-start.27 = (f32[128,384]{1,0:T(8,128)S(1)}, f32[128,384]{1,0:T(8,128)}, u32[]{:S(2)}) copy-start(f32[128,384]{1,0:T(8,128)} %get-tuple-element.85) | copy-start | bytes 589828
  253.7 21.3 %copy-start.26 = (f32[128,384]{1,0:T(8,128)S(1)}, f32[128,384]{1,0:T(8,128)}, u32[]{:S(2)}) copy-start(f32[128,384]{1,0:T(8,128)} %get-tuple-element.86) | copy-start | bytes 589828
  255.2 39.6 %collective-permute-start.54 = (f32[1024,512]{1,0:T(8,128)}, f32[1024,512]{1,0:T(8,128)S(1)}, u32[]{:S(2)}, u32[]{:S(2)}) collective-permute-start(f32[1024,512]{1,0:T(8,128)} %constant_dynamic-slice_fusion), channel_id=1, source_target_pairs={{0,1},{1,0},{2,3},{3,2},{4,5},{5,4},{6,7},{7,6},{8,9},{9,8},{10,11... | collective-permute-start | bytes 6291464 | tf_op jit(solution)/shard_map/ppermute | solution.py:250
  255.7 32.2 %collective-permute-start.32 = (f32[8,64,512]{2,1,0:T(8,128)S(1)}, f32[8,64,512]{2,1,0:T(8,128)S(1)}, u32[]{:S(2)}, u32[]{:S(2)}) collective-permute-start(f32[8,64,512]{2,1,0:T(8,128)S(1)} %constant_dynamic-update-slice_fusion.a), channel_id=1, source_target_pairs={{0,1},{1,0},{2,3},{3,2},{4,5},{5,4},{6,7},{7,6},{8,9},{9,8},{10,11... | collective-permute-start | bytes 3145736 | tf_op jit(solution)/shard_map/ppermute | solution.py:250
  255.7 32.0 %copy-start.13 = (f32[8,64,512]{2,1,0:T(8,128)}, f32[8,64,512]{2,1,0:T(8,128)S(1)}, u32[]{:S(2)}) copy-start(f32[8,64,512]{2,1,0:T(8,128)S(1)} %collective-permute-done.31.f) | copy-start | bytes 3145732
  255.7 32.2 %collective-permute-start.33 = (f32[8,64,512]{2,1,0:T(8,128)S(1)}, f32[8,64,512]{2,1,0:T(8,128)}, u32[]{:S(2)}, u32[]{:S(2)}) collective-permute-start(f32[8,64,512]{2,1,0:T(8,128)S(1)} %collective-permute-done.31.f), channel_id=1, source_target_pairs={{0,1},{1,0},{2,3},{3,2},{4,5},{5,4},{6,7},{7,6},{8,9},{9,8},{10,11... | collective-permute-start | bytes 3145736 | tf_op jit(solution)/shard_map/ppermute | solution.py:250
  256.2 6.9 %collective-permute-start.16 = (f32[128,384]{1,0:T(8,128)S(1)}, f32[128,384]{1,0:T(8,128)S(1)}, u32[]{:S(2)}, u32[]{:S(2)}) collective-permute-start(f32[128,384]{1,0:T(8,128)S(1)} %copy-done.28), channel_id=1, source_target_pairs={{0,2},{1,3},{2,0},{3,1},{4,6},{5,7},{6,4},{7,5},{8,10},{9,11},{10,... | collective-permute-start | bytes 589832 | tf_op jit(solution)/shard_map/ppermute | solution.py:250
  263.1 20.6 %copy-start.30 = (f32[128,384]{1,0:T(8,128)}, f32[128,384]{1,0:T(8,128)S(1)}, u32[]{:S(2)}) copy-start(f32[128,384]{1,0:T(8,128)S(1)} %collective-permute-done.16.q1) | copy-start | bytes 589828
  263.1 11.9 %collective-permute-start.17 = (f32[128,384]{1,0:T(8,128)S(1)}, f32[128,384]{1,0:T(8,128)S(1)}, u32[]{:S(2)}, u32[]{:S(2)}) collective-permute-start(f32[128,384]{1,0:T(8,128)S(1)} %copy-done.27), channel_id=1, source_target_pairs={{0,4},{1,5},{2,6},{3,7},{4,0},{5,1},{6,2},{7,3},{8,12},{9,13},{10,... | collective-permute-start | bytes 589832 | tf_op jit(solution)/shard_map/ppermute | solution.py:250
  275.0 8.6 %collective-permute-start.18 = (f32[128,384]{1,0:T(8,128)S(1)}, f32[128,384]{1,0:T(8,128)S(1)}, u32[]{:S(2)}, u32[]{:S(2)}) collective-permute-start(f32[128,384]{1,0:T(8,128)S(1)} %copy-done.26), channel_id=1, source_target_pairs={{0,6},{1,7},{2,4},{3,5},{4,2},{5,3},{6,0},{7,1},{8,14},{9,15},{10,... | collective-permute-start | bytes 589832 | tf_op jit(solution)/shard_map/ppermute | solution.py:250
  287.8 6.4 %collective-permute-start.52 = (f32[8,512]{1,0:T(8,128)S(1)}, f32[8,512]{1,0:T(8,128)S(1)}, u32[]{:S(2)}, u32[]{:S(2)}) collective-permute-start(f32[8,512]{1,0:T(8,128)S(1)} %copy-done.12), channel_id=1, source_target_pairs={{0,1},{1,0},{2,3},{3,2},{4,5},{5,4},{6,7},{7,6},{8,9},{9,8},{10,11... | collective-permute-start | bytes 49160 | tf_op jit(solution)/shard_map/ppermute | solution.py:250
  (36 other events, 82.2 us)
